TPU v7x, 512 devices: a whole 4x8x8 slice. The times are simulated.
512 devices in a mesh: row: 16 (over z, core), col: 32 (over x, y).
Axes of the slice: x: 4, y: 8, z: 8, core: 2. Of those that a mesh axis runs over, the one named last changes fastest.
Arguments:
- left_vecs: float32 [1024, 53248], P('row', 'col'), may hold values from -0.02734375 to 0.02734375
- left_cot: float32 [1024, 53248], P('row', 'col'), may hold values from -0.02734375 to 0.02734375
- right_vecs: float32 [1024, 53248], P('row', 'col'), may hold values from -0.02734375 to 0.02734375
- right_cot: float32 [1024, 53248], P('row', 'col'), may hold values from -0.02734375 to 0.02734375
- values: float32 [1024], replicated, may hold values from 0.2 to 1
- value_cot: float32 [1024], replicated, may hold values from -8 to 8
Outputs:
- slab_cot: float32 [192, 53248], P('row', 'col')
All inputs are finite; a program needn't handle non-finite values.
Results may differ from a plain program's by a relative error of at most 0.000088.
Values sent between devices are 32-bit elements; how exact they have to be, the bound alone decides.
A program may use at most 64 MiB of HBM per device.

v0:
```python
import math

import jax
import jax.numpy as jnp
from jax import lax
from jax.sharding import PartitionSpec as P

ORDER = 53248
KEEP = 1024
SLAB = 192


broaden = 0.0001


def broadcast(block, axis, source):
    block = jnp.where(lax.axis_index(axis) == source, block, jnp.zeros_like(block))
    return lax.psum(block, axis)


def contract_last(left, right):
    return lax.dot_general(
        left,
        right,
        (((1,), (1,)), ((), ())),
        precision=lax.Precision.HIGHEST,
        preferred_element_type=jnp.float32,
    )


def plain_product(left, right):
    return jnp.dot(left, right, precision=lax.Precision.HIGHEST, preferred_element_type=jnp.float32)


def body(left_vecs, left_cot, right_vecs, right_cot, values, value_cot):
    row_index = lax.axis_index("row")
    width = left_vecs.shape[0]
    keep_total = values.shape[0]
    own_start = row_index * width
    own_values = lax.dynamic_slice_in_dim(values, own_start, width, 0)
    own_cot = lax.dynamic_slice_in_dim(value_cot, own_start, width, 0)
    left_whole, right_whole = (
        lax.all_gather(left_vecs, "row", axis=0, tiled=True),
        lax.all_gather(right_vecs, "row", axis=0, tiled=True),
    )
    gram_left = contract_last(left_whole, left_cot)
    gram_right = contract_last(right_whole, right_cot)
    gram_left, gram_right = lax.psum((gram_left, gram_right), "col")
    left_rows, right_rows = (
        lax.all_to_all(gram_left, "row", split_axis=0, concat_axis=1, tiled=True),
        lax.all_to_all(gram_right, "row", split_axis=0, concat_axis=1, tiled=True),
    )
    squares = values * values
    own_squares = own_values * own_values
    head_left_t, head_cot_t = (
        broadcast(left_vecs[:, :SLAB], "col", 0),
        broadcast(left_cot[:, :SLAB], "col", 0),
    )
    head_left = head_left_t.T
    head_cot = head_cot_t.T
    inverse = 1.0 / own_values
    left_trans = gram_left.T
    right_trans = gram_right.T
    spacing = squares[None, :] - own_squares[:, None]
    factor = spacing / (spacing * spacing + broaden)
    column_ids = lax.broadcasted_iota(jnp.int32, (width, keep_total), 1)
    row_ids = lax.broadcasted_iota(jnp.int32, (width, keep_total), 0)
    diagonal = jnp.where(column_ids == own_start + row_ids, own_cot[:, None], jnp.float32(0.0))
    inner = factor * (left_rows - left_trans) * values[None, :] + diagonal
    inner = inner + own_values[:, None] * factor * (right_rows - right_trans)
    mixing = inner - left_rows / values[None, :] - right_trans / own_values[:, None]
    combined = plain_product(mixing, right_whole) + inverse[:, None] * right_cot
    summed = lax.psum_scatter(
        plain_product(head_left, combined) + plain_product(head_cot * inverse[None, :], right_vecs),
        "row",
        scatter_dimension=0,
        tiled=True,
    )
    return summed * (ORDER / math.sqrt(KEEP))


def solution(mesh):
    in_specs = (P("row", "col"), P("row", "col"), P("row", "col"), P("row", "col"), P(), P())
    out_specs = P("row", "col")
    return jax.shard_map(body, mesh=mesh, in_specs=in_specs, out_specs=out_specs, check_vma=False)
```

profile of v0, /device:TPU:1, one launch (start us, length us, event | category | flops | bytes accessed | tf_op | source)
XLA Modules:
  0.0 523.6 jit_solution(14774238266406027604)
XLA Ops:
  6.5 0.7 all-gather.3.cloned.1.call-update
  7.3 0.0 all-gather.5.cloned.1.call-start
  7.3 0.7 all-gather.5.cloned.1.call-update
  8.0 0.0 all-reduce.9.cloned.1.call-start
  8.1 59.3 %all-gather.3.cloned.1.call-done = f32[1024,1664]{1,0:T(8,128)} async-done(((f32[64,1664]{1,0:T(8,128)}), f32[1024,1664]{1,0:T(8,128)}) %all-gather.3.cloned.1.call-update) | async-done | bytes 6815760 | tf_op jit(solution)/shard_map/all_gather | solution.py:43
  67.4 10.3 %fusion.27 = f32[1024,64]{0,1:T(8,128)} fusion(f32[1024,1664]{1,0:T(8,128)} %all-gather.3.cloned.1.call-done, f32[64,1664]{1,0:T(8,128)} %param.7), kind=kOutput, calls=%fused_computation.38 | convolution fusion | flops 1308622848 | bytes 7503872 | tf_op jit(solution)/shard_map/dot_general | solution.py:22
  77.7 41.8 %all-gather.5.cloned.1.call-done = f32[1024,1664]{1,0:T(8,128)} async-done(((f32[64,1664]{1,0:T(8,128)}), f32[1024,1664]{1,0:T(8,128)}) %all-gather.5.cloned.1.call-update) | async-done | bytes 6815760 | tf_op jit(solution)/shard_map/all_gather | solution.py:44
  119.5 10.3 %fusion.28 = f32[1024,64]{0,1:T(8,128)} fusion(f32[1024,1664]{1,0:T(8,128)} %all-gather.5.cloned.1.call-done, f32[64,1664]{1,0:T(8,128)S(1)} %copy-done.1), kind=kOutput, calls=%fused_computation.39 | convolution fusion | flops 1308622848 | bytes 7503872 | tf_op jit(solution)/shard_map/dot_general | solution.py:22
  129.8 0.0 all-reduce.9.cloned.1.call-update
  129.9 151.6 %all-reduce.9.cloned.1.call-done = (f32[1024,64]{0,1:T(8,128)}, f32[1024,64]{0,1:T(8,128)}) async-done(((f32[1024,64]{0,1:T(8,128)}, f32[1024,64]{0,1:T(8,128)}), (f32[1024,64]{0,1:T(8,128)}, f32[1024,64]{0,1:T(8,128)})) %all-reduce.9.cloned.1.call-update) | async-done | bytes 524304 | tf_op jit(solution)/shard_map/psum | solution.py:48
  281.5 1.2 all_to_all.32
  282.6 0.2 copy.16
  282.8 1.0 reshape.14
  283.9 12.6 %all-to-all-start.1 = ((f32[16,1,4096]{2,1,0:T(1,128)}), f32[16,1,4096]{2,1,0:T(1,128)S(1)}, u32[]{:S(2)}, u32[]{:S(2)}) async-start(f32[16,1,4096]{2,1,0:T(1,128)} %reshape.14), calls=%async_computation.1 | async-start | bytes 524288 | tf_op jit(solution)/shard_map/all_to_all | solution.py:51
  296.5 1.5 slice_select_fusion.1
  298.0 1.1 copy.13
  299.1 1.0 reshape.16
  300.1 8.1 %all-to-all-done.1 = f32[16,1,4096]{2,1,0:T(1,128)S(1)} async-done(((f32[16,1,4096]{2,1,0:T(1,128)}), f32[16,1,4096]{2,1,0:T(1,128)S(1)}, u32[]{:S(2)}, u32[]{:S(2)}) %all-to-all-start.1) | async-done | bytes 262176 | tf_op jit(solution)/shard_map/all_to_all | solution.py:51
  308.2 3.4 all-to-all-start
  311.6 0.2 all-reduce.7.cloned.1.call-start
  311.9 1.5 slice_select_fusion
  313.3 0.0 all-reduce.7.cloned.1.call-update
  313.4 0.8 dynamic_slice.7
  314.1 0.1 fusion.26
  314.2 0.6 broadcast.16
  314.8 1.3 reduce
  316.1 0.2 reshape.15
  316.3 0.2 copy.14
  316.5 0.0 copy-start
  316.5 6.2 %all-to-all-done = f32[16,1,4096]{2,1,0:T(1,128)S(1)} async-done(((f32[16,1,4096]{2,1,0:T(1,128)}), f32[16,1,4096]{2,1,0:T(1,128)S(1)}, u32[]{:S(2)}, u32[]{:S(2)}) %all-to-all-start) | async-done | bytes 262176 | tf_op jit(solution)/shard_map/all_to_all | solution.py:50
  322.7 1.3 reduce.1
  324.0 0.2 reshape.17
  324.3 0.3 copy.10
  324.6 0.2 all_to_all.31
  324.8 6.6 %convolution_add_fusion.1 = f32[64,1664]{1,0:T(8,128)S(1)} fusion(f32[1024,1664]{1,0:T(8,128)} %all-gather.5.cloned.1.call-done, f32[64,1664]{1,0:T(8,128)S(1)} %copy-done.1, f32[64,1024]{1,0:T(8,128)S(1)} %copy.14, f32[1024,64]{0,1:T(8,128)S(1)} %copy-done.2, f32[64,1024]{1,0:T(8,128)S(1)} %all_to_all.31, f32[1024,64]{0,1:T(8,128)S(1)} %copy-done.3, ...), kind=kOutput, calls=%fused_computation.1 | convolution fusion | flops 1310015488 | bytes 8725760 | tf_op jit(solution)/shard_map/dot_general | solution.py:32
  331.4 128.3 %all-reduce.7.cloned.1.call-done = (f32[64,192]{1,0:T(8,128)}, f32[64,192]{1,0:T(8,128)}) async-done(((f32[64,192]{1,0:T(8,128)}, f32[64,192]{1,0:T(8,128)}), (f32[64,192]{1,0:T(8,128)}, f32[64,192]{1,0:T(8,128)})) %all-reduce.7.cloned.1.call-update) | async-done | bytes 98320 | tf_op jit(solution)/shard_map/psum | solution.py:18
  459.7 2.0 fusion.29
  461.8 2.1 convolution_add_fusion
  463.9 34.5 %fusion = f32[16,1664]{1,0:T(8,128)S(1)} fusion(f32[192,1664]{1,0:T(8,128)S(1)} %convolution_add_fusion), kind=kCustom, calls=%all-reduce-scatter | all-reduce-scatter fusion | flops 425985 | bytes 1386496
  498.4 1.3 collective-permute-start.2
  499.7 4.7 collective-permute-start.1
  504.4 3.8 collective-permute-start
  508.2 5.0 collective-permute-start.3
  513.2 1.3 dynamic-slice.4
  515.1 0.6 collective-permute-done.3
  515.7 0.0 collective-permute-done.2
  515.7 0.7 concatenate
  516.4 0.7 dynamic-slice_multiply_fusion
  (16 shorter events, 0.0 us)
Async XLA Ops:
  6.5 113.0 %copy-start.1 = (f32[64,1664]{1,0:T(8,128)S(1)}, f32[64,1664]{1,0:T(8,128)}, u32[]{:S(2)}) copy-start(f32[64,1664]{1,0:T(8,128)} %param.9) | copy-start | bytes 1277956
  6.5 60.8 %all-gather.3.cloned.1.call-start = ((), (), s32[]{:S(2)}) async-start(), calls=%async_computation.2 | async-start | bytes 7241728 | tf_op jit(solution)/shard_map/all_gather | solution.py:43
  7.3 112.2 %all-gather.5.cloned.1.call-start = ((), (), s32[]{:S(2)}) async-start(), calls=%async_computation.3 | async-start | bytes 7241728 | tf_op jit(solution)/shard_map/all_gather | solution.py:44
  8.0 273.5 %all-reduce.9.cloned.1.call-start = ((), (), s32[]{:S(2)}) async-start(), calls=%async_computation.5 | async-start | bytes 1048576 | tf_op jit(solution)/shard_map/psum | solution.py:48
  77.7 235.7 %copy-start.4 = (f32[1024]{0:T(1024)S(1)}, f32[1024]{0:T(1024)}, u32[]{:S(2)}) copy-start(f32[1024]{0:T(1024)} %param.10) | copy-start | bytes 12292
  281.5 43.3 %copy-start.2 = (f32[1024,64]{0,1:T(8,128)S(1)}, f32[1024,64]{0,1:T(8,128)}, u32[]{:S(2)}) copy-start(f32[1024,64]{0,1:T(8,128)} %get-tuple-element.7) | copy-start | bytes 786436
  281.5 43.3 %copy-start.3 = (f32[1024,64]{0,1:T(8,128)S(1)}, f32[1024,64]{0,1:T(8,128)}, u32[]{:S(2)}) copy-start(f32[1024,64]{0,1:T(8,128)} %get-tuple-element.8) | copy-start | bytes 786436
  283.9 24.3 %all-to-all-start.1 = ((f32[16,1,4096]{2,1,0:T(1,128)}), f32[16,1,4096]{2,1,0:T(1,128)S(1)}, u32[]{:S(2)}, u32[]{:S(2)}) async-start(f32[16,1,4096]{2,1,0:T(1,128)} %reshape.14), calls=%async_computation.1 | async-start | bytes 524288 | tf_op jit(solution)/shard_map/all_to_all | solution.py:51
  308.2 14.6 %all-to-all-start = ((f32[16,1,4096]{2,1,0:T(1,128)}), f32[16,1,4096]{2,1,0:T(1,128)S(1)}, u32[]{:S(2)}, u32[]{:S(2)}) async-start(f32[16,1,4096]{2,1,0:T(1,128)} %reshape.16), calls=%async_computation | async-start | bytes 524288 | tf_op jit(solution)/shard_map/all_to_all | solution.py:50
  311.6 148.1 %all-reduce.7.cloned.1.call-start = ((), (), s32[]{:S(2)}) async-start(), calls=%async_computation.4 | async-start | bytes 262144 | tf_op jit(solution)/shard_map/psum | solution.py:18
  316.5 145.3 %copy-start = (f32[64,1664]{1,0:T(8,128)S(1)}, f32[64,1664]{1,0:T(8,128)}, u32[]{:S(2)}) copy-start(f32[64,1664]{1,0:T(8,128)} %param.8) | copy-start | bytes 1277956
  498.4 17.3 %collective-permute-start.2 = (f32[16,1664]{1,0:T(8,128)S(1)}, f32[16,1664]{1,0:T(8,128)S(1)}, u32[]{:S(2)}, u32[]{:S(2)}) collective-permute-start(f32[16,1664]{1,0:T(8,128)S(1)} %fusion), channel_id=1, source_target_pairs={{0,96},{32,128},{64,160},{96,192},{128,224},{160,256},{192,288},{2... | collective-permute-start | bytes 319496
  499.7 16.0 %collective-permute-start.1 = (f32[16,1664]{1,0:T(8,128)S(1)}, f32[16,1664]{1,0:T(8,128)S(1)}, u32[]{:S(2)}, u32[]{:S(2)}) collective-permute-start(f32[16,1664]{1,0:T(8,128)S(1)} %fusion), channel_id=1, source_target_pairs={{0,64},{32,96},{64,128},{96,160},{128,192},{160,224},{192,256},{22... | collective-permute-start | bytes 319496
  504.4 11.3 %collective-permute-start = (f32[16,1664]{1,0:T(8,128)S(1)}, f32[16,1664]{1,0:T(8,128)S(1)}, u32[]{:S(2)}, u32[]{:S(2)}) collective-permute-start(f32[16,1664]{1,0:T(8,128)S(1)} %fusion), channel_id=1, source_target_pairs={{0,32},{32,64},{64,96},{96,128},{128,160},{160,192},{192,224},{224... | collective-permute-start | bytes 319496
  508.2 7.5 %collective-permute-start.3 = (f32[12,1664]{1,0:T(8,128)S(1)}, f32[12,1664]{1,0:T(8,128)S(1)}, u32[]{:S(2)}, u32[]{:S(2)}) collective-permute-start(f32[12,1664]{1,0:T(8,128)S(1)} %slice.8), channel_id=1, source_target_pairs={{0,128},{32,160},{64,192},{96,224},{128,256},{160,288},{192,320},{... | collective-permute-start | bytes 239624
Sparse Core Ops, SparseCore 0:
  9.5 57.8 all-gather.2
  69.5 49.9 all-gather.4
  130.0 151.4 all-reduce.8
  316.1 143.5 all-reduce.6
where the time goes:
time: 524 us
  waiting for transfers between devices  397 us (76%)
  blocking collectives  34.5 us (7%)
  matrix products  31.4 us (6%)
  starting transfers between devices  31.1 us (6%)
  between operations  14 us (3%)
  local copies, waits for them, and re-layouts  8.9 us (2%)
  other arithmetic  6.26 us (1%)
    psum x1, waiting for transfers between devices, body(): gram_left, gram_right = lax.psum((gram_left, gram_right), 'col')  152 us
    psum x1, waiting for transfers between devices, broadcast(): return lax.psum(block, axis)  128 us
    all_gather x1, waiting for transfers between devices, body(): lax.all_gather(left_vecs, 'row', axis=0, tiled=True)  59.3 us
    all_gather x1, waiting for transfers between devices, body(): lax.all_gather(right_vecs, 'row', axis=0, tiled=True)  41.8 us
    unnamed x1, blocking collectives  34.5 us
    dot_general x2, matrix products, contract_last(): lax.dot_general(left, right, (((1,), (1,)), ((), ())), precision=lax.Prec...  20.7 us
    unnamed x4, starting transfers between devices  14.8 us
    all_to_all x1, starting transfers between devices, body(): lax.all_to_all(gram_right, 'row', split_axis=0, concat_axis=1, tiled=True)  12.6 us
  transfers between devices with their start and end apart: 10, of which 7 were waited for; matrix products, arithmetic and copies ran while one was open for 5% of the time, Pallas kernels for 0%

commit v1 on v0

v1 whole, which is shorter than its diff:
```python
import functools
import math

import jax
import jax.numpy as jnp
from jax import lax
from jax.experimental import pallas as pl
from jax.experimental.pallas import tpu as pltpu
from jax.sharding import PartitionSpec as P

ORDER = 53248
KEEP = 1024
SLAB = 192
BROADEN = 0.0001
LANES = 128
F32 = jnp.float32
BF16 = jnp.bfloat16


def split(value):
    high = value.astype(BF16)
    return high, (value - high.astype(F32)).astype(BF16)


def dot_nn(left, right):
    return lax.dot_general(left, right, (((1,), (0,)), ((), ())), preferred_element_type=F32)


def dot_nt(left, right):
    return lax.dot_general(left, right, (((1,), (1,)), ((), ())), preferred_element_type=F32)


def kernel(geo, scale, *refs):
    nx, ny, nz, piece, head_piece, slab, own_cols = geo
    rows_n = 2 * nz
    plane = nx * ny
    keep = nz * LANES
    half = slab // 2
    out_rows = slab // rows_n
    width = own_cols * rows_n
    head_pieces = slab // head_piece
    groups = half // piece
    block = min(256, keep)
    (a_in, b_in, p_in, q_in, values, value_cot, out,
     panels, turned, got, lhs, rhs, p_own, p_other, column, factor,
     heads, head_own, head_x, head_extra, head_slot, head_ring, head_all,
     w_acc, w_part, w_other, rs_src, rs_buf, ar_src, ar_buf, ag_src, w_full,
     low, third, third_other, out_src, out_buf,
     load_sem, a2a_send, a2a_recv, core_send, core_recv, h1_send, h1_recv, h2_send, h2_recv,
     h3_send, h3_recv, rs_send, rs_recv, ar_send, ar_recv, ag_send, ag_recv, o_send, o_recv) = refs

    row = lax.axis_index("row")
    col = lax.axis_index("col")
    z, core = row // 2, row % 2
    x, y = col // ny, col % ny
    other = z * 2 + 1 - core
    along = (1 - core) * y + core * z
    across = (1 - core) * z + core * y
    me = x * ny + along

    def plane_device(index):
        px, pt = index // ny, index % ny
        py = (1 - core) * pt + core * y
        pz = (1 - core) * z + core * pt
        return (pz * 2 + core, px * ny + py)

    def line_device(index):
        py = (1 - core) * y + core * index
        pz = (1 - core) * index + core * z
        return (pz * 2 + core, x * ny + py)

    def remote(src, dst, send, recv, device):
        return pltpu.make_async_remote_copy(
            src_ref=src, dst_ref=dst, send_sem=send, recv_sem=recv,
            device_id=device, device_id_type=pl.DeviceIdType.MESH)

    def loop(count, step, first=0):
        def run(i, carry):
            step(i)
            return carry
        lax.fori_loop(first, count, run, 0)

    barrier = pltpu.get_barrier_semaphore()

    def greet(device):
        pl.semaphore_signal(barrier, inc=1, device_id=device, device_id_type=pl.DeviceIdType.MESH)

    loop(rows_n, lambda k: greet((lax.rem(row + k, rows_n), col)), 1)
    loop(plane, lambda k: greet(plane_device(lax.rem(me + k, plane))), 1)
    loop(nz, lambda k: greet(line_device(lax.rem(across + k, nz))), 1)

    loads = [
        pltpu.make_async_copy(source, panels.at[i // 2, pl.ds(64 * (i % 2), 64)], load_sem.at[i])
        for i, source in enumerate((a_in, b_in, p_in, q_in))
    ]
    for copy in loads:
        copy.start()
    got[:, :, own_cols:, :] = jnp.zeros((2, rows_n, LANES - own_cols, LANES), F32)

    def turn(pair):
        loads[2 * pair].wait()
        loads[2 * pair + 1].wait()
        for tile in range(width // LANES):
            turned[pair, tile * LANES:(tile + 1) * LANES, :] = panels[pair, :, tile * LANES:(tile + 1) * LANES].T

    turn(0)
    turn(1)
    pl.semaphore_wait(barrier, rows_n - 1 + plane - 1 + nz - 1)

    def a2a(pair, k):
        to = lax.rem(row + k, rows_n)
        return remote(
            turned.at[pair, pl.ds(pl.multiple_of(to * own_cols, 8), own_cols)],
            got.at[pair, row, pl.ds(0, own_cols)],
            a2a_send.at[pair, k], a2a_recv.at[pair, row], (to, col))

    def a2a_from(pair, k):
        source = lax.rem(row + k, rows_n)
        return remote(
            turned.at[pair, pl.ds(0, own_cols)], got.at[pair, source, pl.ds(0, own_cols)],
            a2a_send.at[pair, k], a2a_recv.at[pair, source], (source, col))

    first_col = col == 0
    head_core = core == 0
    carries = jnp.logical_and(head_core, col < head_pieces)
    lane = lax.broadcasted_iota(jnp.int32, (slab, LANES), 1)

    def merge(left, right, lanes):
        return (jnp.where(lanes < 64, left, pltpu.roll(right, 64, 1)),
                jnp.where(lanes < 64, pltpu.roll(left, 64, 1), right))

    to_core0 = remote(turned.at[0, pl.ds(0, slab)], head_x, core_send.at[0], core_recv.at[0], (other, col))

    def h1(p):
        return remote(head_own.at[pl.ds(pl.multiple_of(p * head_piece, 8), head_piece)], head_slot,
                      h1_send.at[p], h1_recv.at[0], (row, p))

    def h2(k):
        to = lax.rem(z + k, nz)
        return remote(head_slot, head_ring.at[z], h2_send.at[k], h2_recv.at[z], (to * 2 + core, col))

    def h2_from(k):
        source = lax.rem(z + k, nz)
        return remote(head_slot, head_ring.at[source], h2_send.at[k], h2_recv.at[source], (source * 2 + core, col))

    def head_rows(p):
        return head_all.at[:, pl.ds(pl.multiple_of(p * head_piece, 8), head_piece)]

    def h3(k):
        return remote(head_ring, head_rows(col), h3_send.at[k], h3_recv.at[col], (row, lax.rem(col + k, plane)))

    def h3_from(p):
        return remote(head_ring, head_rows(p), h3_send.at[0], h3_recv.at[p], (row, p))

    @pl.when(jnp.logical_and(first_col, core == 1))
    def _():
        to_core0.start()

    @pl.when(jnp.logical_and(first_col, head_core))
    def _():
        to_core0.wait_recv()
        head, head_cot = merge(turned[0, 0:slab, :], head_x[...], lane)
        head_own[...] = head
        here = pl.ds(pl.multiple_of(z * LANES, LANES), LANES)
        head_extra[...] = head * value_cot[:, here] + head_cot / values[:, here]
        loop(head_pieces, lambda p: h1(p).start(), 1)
        head_slot[...] = head[0:head_piece]

    loop(rows_n, lambda k: a2a(0, k).start(), 1)
    loop(rows_n, lambda k: a2a(1, k).start(), 1)
    for pair in range(2):
        got[pair, row, 0:own_cols, :] = turned[pair, pl.ds(pl.multiple_of(row * own_cols, 8), own_cols), :]

    @pl.when(carries)
    def _():
        @pl.when(jnp.logical_not(first_col))
        def _():
            h1(col).wait_recv()
        loop(nz, lambda k: h2(k).start(), 1)
        head_ring[z] = head_slot[...]

    for j in range(nz):
        here = slice(j * LANES, (j + 1) * LANES)
        column[here, :] = jnp.broadcast_to(values[:, here] * values[:, here], (LANES, LANES)).T

    def gaps(j):
        here = pl.ds(pl.multiple_of(j * LANES, LANES), LANES)
        across_values = values[:, here]
        spacing = across_values * across_values - column[...]
        factor[:, here] = spacing / (spacing * spacing + BROADEN)

    loop(nz, gaps)

    @pl.when(carries)
    def _():
        loop(nz, lambda k: h2_from(k).wait_recv(), 1)
        loop(plane, lambda k: h3(k).start(), 1)
        head_all[:, pl.ds(pl.multiple_of(col * head_piece, 8), head_piece), :] = head_ring[...]

    def prepare(pair):
        loop(rows_n, lambda k: a2a_from(pair, k).wait_recv(), 1)
        lanes = lax.broadcasted_iota(jnp.int32, (LANES, LANES), 1)
        for j in range(nz):
            first, second = merge(got[pair, 2 * j], got[pair, 2 * j + 1], lanes)
            here = slice(j * LANES, (j + 1) * LANES)
            if pair == 1:
                p_own[:, here] = first
            for at, value in ((0, second), (LANES, first)):
                high, rest = split(value)
                rhs[pair, at:at + LANES, here] = high
                rhs[pair, 256 + at:256 + at + LANES, here] = high
                rhs[pair, 512 + at:512 + at + LANES, here] = rest
            for at, value in ((0, first.T), (LANES, -second.T)):
                high, rest = split(value)
                lhs[here, at:at + LANES] = high
                lhs[here, 256 + at:256 + at + LANES] = rest
                lhs[here, 512 + at:512 + at + LANES] = high

    def through(stacked, count, high, rest, dot):
        both = dot(stacked, high)
        return both[:count] + both[count:] + dot(stacked[:count], rest)

    def low_rank(which, pair, at):
        value = through(heads[which], slab, rhs[pair, at:at + LANES, :], rhs[pair, 512 + at:512 + at + LANES, :], dot_nt)
        high, rest = split(value)
        low[0:slab, :] = high
        low[slab:, :] = rest
        return value

    def columns(pair, j):
        here = pl.ds(pl.multiple_of(j * block, block), block)
        right = rhs[pair, :, here]
        both = jnp.zeros((2 * slab, block), F32)
        total = jnp.zeros((slab, block), F32)
        for i in range(keep // block):
            there = slice(i * block, (i + 1) * block)
            high, rest = split(factor[there, here] * dot_nn(lhs[there, :], right))
            both = both + dot_nn(heads[pair, :, there], high)
            total = total + dot_nn(heads[pair, 0:slab, there], rest)
        total = total + both[:slab] + both[slab:]
        at = LANES * pair
        outer = through(low[...], slab, right[at:at + LANES], right[512 + at:512 + at + LANES], dot_nn)
        if pair == 0:
            w_acc[:, here] = total * values[:, here] - outer / values[:, here]
            return
        total = w_acc[:, here] + total - outer
        for t in range(block // LANES):
            for h in range(2):
                for g in range(groups):
                    start = h * half + g * piece
                    w_part[h, g * nz + j * (block // LANES) + t] = total[start:start + piece, t * LANES:(t + 1) * LANES]

    prepare(0)

    to_core1 = remote(head_all, head_all, core_send.at[1], core_recv.at[1], (other, col))

    @pl.when(head_core)
    def _():
        def arrived(p):
            @pl.when(p != col)
            def _():
                h3_from(p).wait_recv()
        loop(head_pieces, arrived)
        to_core1.start()

    @pl.when(core == 1)
    def _():
        to_core1.wait_recv()

    for j in range(nz):
        here = slice(j * LANES, (j + 1) * LANES)
        head = head_all[j]
        for which, value in enumerate((head, head * values[:, here], head / values[:, here])):
            high, rest = split(value)
            heads[which, 0:slab, here] = high
            heads[which, slab:, here] = rest

    low_rank(0, 0, LANES)
    loop(keep // block, functools.partial(columns, 0))
    prepare(1)
    third[...] = low_rank(2, 1, 0)
    p_swap = remote(p_own, p_other, core_send.at[2], core_recv.at[2], (other, col))
    third_swap = remote(third.at[pl.ds(pl.multiple_of((1 - core) * half, 8), half)], third_other,
                        core_send.at[3], core_recv.at[3], (other, col))
    p_swap.start()
    third_swap.start()
    loop(keep // block, functools.partial(columns, 1))

    @pl.when(jnp.logical_and(first_col, head_core))
    def _():
        for h in range(2):
            for g in range(groups):
                start = h * half + g * piece
                w_part[h, g * nz + z] = w_part[h, g * nz + z] + head_extra[start:start + piece, :]

    w_swap = remote(w_part.at[1 - core], w_other, core_send.at[4], core_recv.at[4], (other, col))
    w_swap.start()
    w_swap.wait_recv()
    rs_src[...] = w_part[core] + w_other[...]

    def rs(k):
        to = lax.rem(me + k, plane)
        return remote(rs_src.at[to], rs_buf.at[me], rs_send.at[k], rs_recv.at[me], plane_device(to))

    def rs_from(k):
        source = lax.rem(me + k, plane)
        return remote(rs_src.at[source], rs_buf.at[source], rs_send.at[k], rs_recv.at[source], plane_device(source))

    loop(plane, lambda k: rs(k).start(), 1)
    rs_buf[me] = rs_src[me]
    loop(plane, lambda k: rs_from(k).wait_recv(), 1)
    ar_src[...] = jnp.sum(rs_buf[...], axis=0)

    def ar(k):
        to = lax.rem(across + k, nz)
        return remote(ar_src, ar_buf.at[across], ar_send.at[k], ar_recv.at[across], line_device(to))

    def ar_from(k):
        source = lax.rem(across + k, nz)
        return remote(ar_src, ar_buf.at[source], ar_send.at[k], ar_recv.at[source], line_device(source))

    loop(nz, lambda k: ar(k).start(), 1)
    ar_buf[across] = ar_src[...]
    loop(nz, lambda k: ar_from(k).wait_recv(), 1)
    ag_src[...] = jnp.sum(ar_buf[...], axis=0)

    def ag(k):
        to = lax.rem(me + k, plane)
        return remote(ag_src, w_full.at[me], ag_send.at[k], ag_recv.at[me], plane_device(to))

    def ag_from(k):
        source = lax.rem(me + k, plane)
        return remote(ag_src, w_full.at[source], ag_send.at[k], ag_recv.at[source], plane_device(source))

    loop(plane, lambda k: ag(k).start(), 1)
    w_full[me] = ag_src[...]
    p_swap.wait_recv()
    third_swap.wait_recv()
    loop(plane, lambda k: ag_from(k).wait_recv(), 1)

    mine = jnp.zeros((half, LANES), F32)
    theirs = jnp.zeros((half, LANES), F32)
    for j in range(nz):
        here = slice(j * LANES, (j + 1) * LANES)
        high, rest = split(jnp.concatenate([w_full[g * nz + j] for g in range(groups)], axis=0))
        stacked = jnp.concatenate([high, rest], axis=0)
        mine = mine + through(stacked, half, rhs[1, LANES:256, here], rhs[1, 640:768, here], dot_nt)
        theirs = theirs + through(stacked, half, *split(p_other[:, here]), dot_nt)
    mine = (mine + third[pl.ds(pl.multiple_of(core * half, 8), half), :]) * scale
    theirs = (theirs + third_other[...]) * scale
    for i in range(nz):
        for at, value in ((core, mine), (1 - core, theirs)):
            out_src[i, at] = jnp.pad(value[i * out_rows:(i + 1) * out_rows], ((0, 16 - out_rows), (0, 0)))

    def send_out(i):
        to = core * nz + i
        return remote(out_src.at[i], out_buf.at[z], o_send.at[i], o_recv.at[z], (to, col))

    def out_from(i):
        source = 2 * i + row // nz
        return remote(out_src.at[i], out_buf.at[i], o_send.at[i], o_recv.at[i], (source, col))

    def each_out(step):
        def run(i):
            @pl.when(core * nz + i != row)
            def _():
                step(send_out(i))
        loop(nz, run)

    each_out(lambda copy: copy.start())

    @pl.when(core == row // nz)
    def _():
        out_buf[z] = out_src[lax.rem(row, nz)]

    def out_arrived(i):
        @pl.when(2 * i + row // nz != row)
        def _():
            out_from(i).wait_recv()
    loop(nz, out_arrived)
    for i in range(nz):
        for c in range(2):
            start = (2 * i + c) * own_cols
            out[:, start:start + own_cols] = out_buf[i, c, 0:out_rows, 0:own_cols]

    each_out(lambda copy: copy.wait_send())
    loop(rows_n, lambda k: a2a(0, k).wait_send(), 1)
    loop(rows_n, lambda k: a2a(1, k).wait_send(), 1)
    loop(plane, lambda k: rs(k).wait_send(), 1)
    loop(nz, lambda k: ar(k).wait_send(), 1)
    loop(plane, lambda k: ag(k).wait_send(), 1)
    p_swap.wait_send()
    third_swap.wait_send()
    w_swap.wait_send()

    @pl.when(jnp.logical_and(first_col, core == 1))
    def _():
        to_core0.wait_send()

    @pl.when(jnp.logical_and(first_col, head_core))
    def _():
        loop(head_pieces, lambda p: h1(p).wait_send(), 1)

    @pl.when(carries)
    def _():
        loop(nz, lambda k: h2(k).wait_send(), 1)
        loop(plane, lambda k: h3(k).wait_send(), 1)

    @pl.when(head_core)
    def _():
        to_core1.wait_send()


def body(nx, ny, nz, slab, scale, left_vecs, left_cot, right_vecs, right_cot, values, value_cot):
    rows_n, plane, keep, width = 2 * nz, nx * ny, values.shape[0], left_vecs.shape[1]
    own_cols, half = width // rows_n, slab // 2
    piece = half // (plane // nz)
    head_piece = -(-(-(-slab // plane)) // 8) * 8
    pieces = (plane, piece, LANES)
    dma = pltpu.SemaphoreType.DMA
    scratch = [
        pltpu.VMEM((2, LANES, width), F32),
        pltpu.VMEM((2, width, LANES), F32),
        pltpu.VMEM((2, rows_n, LANES, LANES), F32),
        pltpu.VMEM((keep, 768), BF16),
        pltpu.VMEM((2, 768, keep), BF16),
        pltpu.VMEM((LANES, keep), F32),
        pltpu.VMEM((LANES, keep), F32),
        pltpu.VMEM((keep, LANES), F32),
        pltpu.VMEM((keep, keep), F32),
        pltpu.VMEM((3, 2 * slab, keep), BF16),
        pltpu.VMEM((slab, LANES), F32),
        pltpu.VMEM((slab, LANES), F32),
        pltpu.VMEM((slab, LANES), F32),
        pltpu.VMEM((head_piece, LANES), F32),
        pltpu.VMEM((nz, head_piece, LANES), F32),
        pltpu.VMEM((nz, slab, LANES), F32),
        pltpu.VMEM((slab, keep), F32),
        pltpu.VMEM((2,) + pieces, F32),
        pltpu.VMEM(pieces, F32),
        pltpu.VMEM(pieces, F32),
        pltpu.VMEM(pieces, F32),
        pltpu.VMEM((piece, LANES), F32),
        pltpu.VMEM((nz, piece, LANES), F32),
        pltpu.VMEM((piece, LANES), F32),
        pltpu.VMEM(pieces, F32),
        pltpu.VMEM((2 * slab, LANES), BF16),
        pltpu.VMEM((slab, LANES), F32),
        pltpu.VMEM((half, LANES), F32),
        pltpu.VMEM((nz, 2, 16, LANES), F32),
        pltpu.VMEM((nz, 2, 16, LANES), F32),
        dma((4,)), dma((2, rows_n)), dma((2, rows_n)), dma((5,)), dma((5,)),
        dma((plane,)), dma((1,)), dma((nz,)), dma((nz,)), dma((plane,)), dma((plane,)),
        dma((plane,)), dma((plane,)), dma((nz,)), dma((nz,)), dma((plane,)), dma((plane,)),
        dma((nz,)), dma((nz,)),
    ]
    vmem, anywhere = pl.BlockSpec(memory_space=pltpu.VMEM), pl.BlockSpec(memory_space=pl.ANY)
    return pl.pallas_call(
        functools.partial(kernel, (nx, ny, nz, piece, head_piece, slab, own_cols), scale),
        out_shape=jax.ShapeDtypeStruct((slab // rows_n, width), F32),
        in_specs=[anywhere] * 4 + [vmem] * 2,
        out_specs=vmem,
        scratch_shapes=scratch,
        compiler_params=pltpu.CompilerParams(
            collective_id=0, has_side_effects=True, vmem_limit_bytes=56 * 1024 * 1024),
        cost_estimate=pl.CostEstimate(flops=12 * 2**30, bytes_accessed=2 * 2**20, transcendentals=0),
    )(left_vecs, left_cot, right_vecs, right_cot, values[None, :], value_cot[None, :])


def build(mesh, nx, ny, nz, slab, scale):
    panel = P("row", "col")
    return jax.shard_map(
        functools.partial(body, nx, ny, nz, slab, scale), mesh=mesh,
        in_specs=(panel, panel, panel, panel, P(), P()), out_specs=panel, check_vma=False)


def solution(mesh):
    return build(mesh, 4, 8, 8, SLAB, ORDER / math.sqrt(KEEP))
```

time: 524 us -> 123 us (0.23)
  waiting for transfers between devices: 397 us -> 0 us
  Pallas kernels: 0 us -> 121 us
  blocking collectives: 34.5 us -> 0 us
  matrix products: 31.4 us -> 0 us
  starting transfers between devices: 31.1 us -> 0 us
  between operations: 14 us -> 0.01 us
  local copies, waits for them, and re-layouts: 8.9 us -> 1.55 us
  other arithmetic: 6.26 us -> 0 us
    psum x2 -> x0, waiting for transfers between devices: 280 us -> none  [the longest x1 152 us: body(): gram_left, gram_right = lax.psum((gram_left, gram_right), 'col')]
    pallas_call x0 -> x1, Pallas kernels: none -> 121 us  [body(): pl.pallas_call(functools.partial(kernel, (nx, ny, nz, piece, head_piece,...]
    all_gather x2 -> x0, waiting for transfers between devices: 101 us -> none  [the longest x1 59.3 us: body(): lax.all_gather(left_vecs, 'row', axis=0, tiled=True)]
    unnamed x1 -> x0, blocking collectives: 34.5 us -> none
    dot_general x5 -> x0, matrix products: 31.4 us -> none  [the longest x2 20.7 us: contract_last(): lax.dot_general(left, right, (((1,), (1,)), ((), ())), precision=lax.Prec...]
    all_to_all x2 -> x0, starting transfers between devices: 16.1 us -> none  [the longest x1 12.6 us: body(): lax.all_to_all(gram_right, 'row', split_axis=0, concat_axis=1, tiled=True)]
    unnamed x4 -> x0, starting transfers between devices: 14.8 us -> none
    all_to_all x2 -> x0, waiting for transfers between devices: 14.3 us -> none  [the longest x1 8.07 us: body(): lax.all_to_all(gram_right, 'row', split_axis=0, concat_axis=1, tiled=True)]
  transfers between devices with their start and end apart: 10 -> 0, of which waited for: 7 -> 0; matrix products, arithmetic and copies ran while one was open for 5% -> 0% of each run, Pallas kernels for 0% -> 0%
where the time goes in v1:
time: 123 us
  Pallas kernels  121 us (98%)
  local copies, waits for them, and re-layouts  1.55 us (1%)
    pallas_call x1, Pallas kernels, body(): pl.pallas_call(functools.partial(kernel, (nx, ny, nz, piece, head_piece,...  121 us

profile of v1, /device:TPU:1, one launch (start us, length us, event | category | flops | bytes accessed | tf_op | source)
XLA Modules:
  0.0 122.7 jit_solution(14656881654083266666)
XLA Ops:
  0.0 121.2 %shard_map.64 = f32[12,1664]{1,0:T(8,128)} custom-call(f32[64,1664]{1,0:T(8,128)} %refs_0_.1, f32[64,1664]{1,0:T(8,128)} %refs_1_.1, f32[64,1664]{1,0:T(8,128)} %refs_2_.1, f32[64,1664]{1,0:T(8,128)} %refs_3_.1, f32[1,1024]{1,0:T(1,128)} %bitcast.2, f32[1,1024]{1,0:T(1,128)} %bitcast.3), custom_call_target="tpu_custom_call" | custom-call | flops 12884901888 | bytes 2097152 | tf_op jit(solution)/shard_map/pallas_call | solution.py:458
  121.2 1.5 %copy.8 = f32[12,1664]{1,0:T(8,128)} copy(f32[12,1664]{1,0:T(8,128)} %shard_map.64) | data formatting | bytes 159744

commit v2 on v1

--- a/solution.py
+++ b/solution.py
@@ -80,6 +80,12 @@
             return carry
         lax.fori_loop(first, count, run, 0)
 
+    sent = []
+
+    def settle():
+        for step in sent:
+            step()
+
     barrier = pltpu.get_barrier_semaphore()
 
     def greet(device):
@@ -152,9 +158,22 @@
     def h3_from(p):
         return remote(head_ring, head_rows(p), h3_send.at[0], h3_recv.at[p], (row, p))
 
+    far_first = [half_way + sign * step for half_way in (rows_n // 2,) for step in range(half_way) for sign in (1, -1)]
+    far_first = [k for i, k in enumerate(far_first) if k not in far_first[:i]]
+    order = [(pair, k) for pair in range(2) for k in far_first]
+    window = min(6, len(far_first) // 2)
+
+    def issue(first, last):
+        for i in range(first, min(last, len(order))):
+            if window <= i < 2 * window:
+                a2a(*order[i - window]).wait_send()
+            a2a(*order[i]).start()
+
     @pl.when(jnp.logical_and(first_col, core == 1))
     def _():
         to_core0.start()
+
+    issue(0, window)
 
     @pl.when(jnp.logical_and(first_col, head_core))
     def _():
@@ -166,8 +185,10 @@
         loop(head_pieces, lambda p: h1(p).start(), 1)
         head_slot[...] = head[0:head_piece]
 
-    loop(rows_n, lambda k: a2a(0, k).start(), 1)
-    loop(rows_n, lambda k: a2a(1, k).start(), 1)
+    @pl.when(jnp.logical_and(first_col, core == 1))
+    def _():
+        to_core0.wait_send()
+
     for pair in range(2):
         got[pair, row, 0:own_cols, :] = turned[pair, pl.ds(pl.multiple_of(row * own_cols, 8), own_cols), :]
 
@@ -179,6 +200,22 @@
         loop(nz, lambda k: h2(k).start(), 1)
         head_ring[z] = head_slot[...]
 
+    issue(window, 2 * window)
+
+    @pl.when(carries)
+    def _():
+        loop(nz, lambda k: h2_from(k).wait_recv(), 1)
+        loop(plane, lambda k: h3(k).start(), 1)
+        head_all[:, pl.ds(pl.multiple_of(col * head_piece, 8), head_piece), :] = head_ring[...]
+
+    issue(2 * window, len(order))
+
+    def a2a_sent():
+        for item in order[window:]:
+            a2a(*item).wait_send()
+
+    sent.append(a2a_sent)
+
     for j in range(nz):
         here = slice(j * LANES, (j + 1) * LANES)
         column[here, :] = jnp.broadcast_to(values[:, here] * values[:, here], (LANES, LANES)).T
@@ -191,11 +228,17 @@
 
     loop(nz, gaps)
 
-    @pl.when(carries)
-    def _():
-        loop(nz, lambda k: h2_from(k).wait_recv(), 1)
-        loop(plane, lambda k: h3(k).start(), 1)
-        head_all[:, pl.ds(pl.multiple_of(col * head_piece, 8), head_piece), :] = head_ring[...]
+    def head_sent():
+        @pl.when(jnp.logical_and(first_col, head_core))
+        def _():
+            loop(head_pieces, lambda p: h1(p).wait_send(), 1)
+
+        @pl.when(carries)
+        def _():
+            loop(nz, lambda k: h2(k).wait_send(), 1)
+            loop(plane, lambda k: h3(k).wait_send(), 1)
+
+    sent.append(head_sent)
 
     def prepare(pair):
         loop(rows_n, lambda k: a2a_from(pair, k).wait_recv(), 1)
@@ -267,6 +310,13 @@
     def _():
         to_core1.wait_recv()
 
+    def head_core_sent():
+        @pl.when(head_core)
+        def _():
+            to_core1.wait_send()
+
+    sent.append(head_core_sent)
+
     for j in range(nz):
         here = slice(j * LANES, (j + 1) * LANES)
         head = head_all[j]
@@ -284,6 +334,7 @@
                         core_send.at[3], core_recv.at[3], (other, col))
     p_swap.start()
     third_swap.start()
+    sent.extend((p_swap.wait_send, third_swap.wait_send))
     loop(keep // block, functools.partial(columns, 1))
 
     @pl.when(jnp.logical_and(first_col, head_core))
@@ -295,6 +346,7 @@
 
     w_swap = remote(w_part.at[1 - core], w_other, core_send.at[4], core_recv.at[4], (other, col))
     w_swap.start()
+    sent.append(w_swap.wait_send)
     w_swap.wait_recv()
     rs_src[...] = w_part[core] + w_other[...]
 
@@ -307,6 +359,7 @@
         return remote(rs_src.at[source], rs_buf.at[source], rs_send.at[k], rs_recv.at[source], plane_device(source))
 
     loop(plane, lambda k: rs(k).start(), 1)
+    sent.append(lambda: loop(plane, lambda k: rs(k).wait_send(), 1))
     rs_buf[me] = rs_src[me]
     loop(plane, lambda k: rs_from(k).wait_recv(), 1)
     ar_src[...] = jnp.sum(rs_buf[...], axis=0)
@@ -320,6 +373,7 @@
         return remote(ar_src, ar_buf.at[source], ar_send.at[k], ar_recv.at[source], line_device(source))
 
     loop(nz, lambda k: ar(k).start(), 1)
+    sent.append(lambda: loop(nz, lambda k: ar(k).wait_send(), 1))
     ar_buf[across] = ar_src[...]
     loop(nz, lambda k: ar_from(k).wait_recv(), 1)
     ag_src[...] = jnp.sum(ar_buf[...], axis=0)
@@ -333,6 +387,7 @@
         return remote(ag_src, w_full.at[source], ag_send.at[k], ag_recv.at[source], plane_device(source))
 
     loop(plane, lambda k: ag(k).start(), 1)
+    sent.append(lambda: loop(plane, lambda k: ag(k).wait_send(), 1))
     w_full[me] = ag_src[...]
     p_swap.wait_recv()
     third_swap.wait_recv()
@@ -384,31 +439,7 @@
             out[:, start:start + own_cols] = out_buf[i, c, 0:out_rows, 0:own_cols]
 
     each_out(lambda copy: copy.wait_send())
-    loop(rows_n, lambda k: a2a(0, k).wait_send(), 1)
-    loop(rows_n, lambda k: a2a(1, k).wait_send(), 1)
-    loop(plane, lambda k: rs(k).wait_send(), 1)
-    loop(nz, lambda k: ar(k).wait_send(), 1)
-    loop(plane, lambda k: ag(k).wait_send(), 1)
-    p_swap.wait_send()
-    third_swap.wait_send()
-    w_swap.wait_send()
-
-    @pl.when(jnp.logical_and(first_col, core == 1))
-    def _():
-        to_core0.wait_send()
-
-    @pl.when(jnp.logical_and(first_col, head_core))
-    def _():
-        loop(head_pieces, lambda p: h1(p).wait_send(), 1)
-
-    @pl.when(carries)
-    def _():
-        loop(nz, lambda k: h2(k).wait_send(), 1)
-        loop(plane, lambda k: h3(k).wait_send(), 1)
-
-    @pl.when(head_core)
-    def _():
-        to_core1.wait_send()
+    settle()
 
 
 def body(nx, ny, nz, slab, scale, left_vecs, left_cot, right_vecs, right_cot, values, value_cot):

time: 123 us -> 98.9 us (0.80)
  Pallas kernels: 121 us -> 97.1 us
    pallas_call x1, Pallas kernels: 121 us -> 97.1 us  [body(): pl.pallas_call(functools.partial(kernel, (nx, ny, nz, piece, head_piece,...]
where the time goes in v2:
time: 98.9 us; the launch traced here: 98.7 us
  Pallas kernels  97.1 us (98%)
  local copies, waits for them, and re-layouts  1.55 us (2%)
    pallas_call x1, Pallas kernels, body(): pl.pallas_call(functools.partial(kernel, (nx, ny, nz, piece, head_piece,...  97.1 us

profile of v2, /device:TPU:1, one launch (start us, length us, event | category | flops | bytes accessed | tf_op | source)
XLA Modules:
  0.0 98.7 jit_solution(14385224288070758311)
XLA Ops:
  0.0 97.1 %shard_map.64 = f32[12,1664]{1,0:T(8,128)} custom-call(f32[64,1664]{1,0:T(8,128)} %refs_0_.1, f32[64,1664]{1,0:T(8,128)} %refs_1_.1, f32[64,1664]{1,0:T(8,128)} %refs_2_.1, f32[64,1664]{1,0:T(8,128)} %refs_3_.1, f32[1,1024]{1,0:T(1,128)} %bitcast.2, f32[1,1024]{1,0:T(1,128)} %bitcast.3), custom_call_target="tpu_custom_call" | custom-call | flops 12884901888 | bytes 2097152 | tf_op jit(solution)/shard_map/pallas_call | solution.py:489
  97.1 1.5 %copy.8 = f32[12,1664]{1,0:T(8,128)} copy(f32[12,1664]{1,0:T(8,128)} %shard_map.64) | data formatting | bytes 159744

commit v3 on v2

--- a/solution.py
+++ b/solution.py
@@ -30,7 +30,7 @@
     return lax.dot_general(left, right, (((1,), (1,)), ((), ())), preferred_element_type=F32)
 
 
-def kernel(geo, scale, *refs):
+def kernel(geo, *refs):
     nx, ny, nz, piece, head_piece, slab, own_cols = geo
     rows_n = 2 * nz
     plane = nx * ny
@@ -40,12 +40,12 @@
     width = own_cols * rows_n
     head_pieces = slab // head_piece
     groups = half // piece
-    block = min(256, keep)
+    block = keep // 2
     (a_in, b_in, p_in, q_in, values, value_cot, out,
      panels, turned, got, lhs, rhs, p_own, p_other, column, factor,
      heads, head_own, head_x, head_extra, head_slot, head_ring, head_all,
      w_acc, w_part, w_other, rs_src, rs_buf, ar_src, ar_buf, ag_src, w_full,
-     low, third, third_other, out_src, out_buf,
+     sym_high, sym_rest, low, third, third_other, out_src, out_buf,
      load_sem, a2a_send, a2a_recv, core_send, core_recv, h1_send, h1_recv, h2_send, h2_recv,
      h3_send, h3_recv, rs_send, rs_recv, ar_send, ar_recv, ag_send, ag_recv, o_send, o_recv) = refs
 
@@ -80,6 +80,18 @@
             return carry
         lax.fori_loop(first, count, run, 0)
 
+    line_order = sorted(range(1, nz), key=lambda d: -min(d, nz - d))
+    plane_order = sorted(
+        ((dx, dt) for dx in range(nx) for dt in range(ny) if dx or dt),
+        key=lambda at: -min(at[0], nx - at[0]) - min(at[1], ny - at[1]))
+    row_order = [(0, 0)] + [(d, c) for d in line_order for c in range(2)]
+
+    def around(dx, dt):
+        return lax.rem(x + dx, nx) * ny + lax.rem(along + dt, ny)
+
+    def row_target(d, c):
+        return lax.rem(z + d, nz) * 2 + c if d else other
+
     sent = []
 
     def settle():
@@ -91,9 +103,12 @@
     def greet(device):
         pl.semaphore_signal(barrier, inc=1, device_id=device, device_id_type=pl.DeviceIdType.MESH)
 
-    loop(rows_n, lambda k: greet((lax.rem(row + k, rows_n), col)), 1)
-    loop(plane, lambda k: greet(plane_device(lax.rem(me + k, plane))), 1)
-    loop(nz, lambda k: greet(line_device(lax.rem(across + k, nz))), 1)
+    for dx, dt in plane_order:
+        greet(plane_device(around(dx, dt)))
+    for d in line_order:
+        greet(line_device(lax.rem(across + d, nz)))
+    for d, c in row_order:
+        greet((row_target(d, c), col))
 
     loads = [
         pltpu.make_async_copy(source, panels.at[i // 2, pl.ds(64 * (i % 2), 64)], load_sem.at[i])
@@ -113,18 +128,17 @@
     turn(1)
     pl.semaphore_wait(barrier, rows_n - 1 + plane - 1 + nz - 1)
 
-    def a2a(pair, k):
-        to = lax.rem(row + k, rows_n)
+    def a2a(pair, d, c):
+        to = row_target(d, c)
         return remote(
             turned.at[pair, pl.ds(pl.multiple_of(to * own_cols, 8), own_cols)],
             got.at[pair, row, pl.ds(0, own_cols)],
-            a2a_send.at[pair, k], a2a_recv.at[pair, row], (to, col))
-
-    def a2a_from(pair, k):
-        source = lax.rem(row + k, rows_n)
+            a2a_send.at[pair, 2 * d + c], a2a_recv.at[pair, row], (to, col))
+
+    def a2a_from(pair, source):
         return remote(
             turned.at[pair, pl.ds(0, own_cols)], got.at[pair, source, pl.ds(0, own_cols)],
-            a2a_send.at[pair, k], a2a_recv.at[pair, source], (source, col))
+            a2a_send.at[pair, 0], a2a_recv.at[pair, source], (source, col))
 
     first_col = col == 0
     head_core = core == 0
@@ -158,10 +172,8 @@
     def h3_from(p):
         return remote(head_ring, head_rows(p), h3_send.at[0], h3_recv.at[p], (row, p))
 
-    far_first = [half_way + sign * step for half_way in (rows_n // 2,) for step in range(half_way) for sign in (1, -1)]
-    far_first = [k for i, k in enumerate(far_first) if k not in far_first[:i]]
-    order = [(pair, k) for pair in range(2) for k in far_first]
-    window = min(6, len(far_first) // 2)
+    order = [(pair, d, c) for pair in range(2) for d, c in row_order]
+    window = min(6, len(row_order) // 2)
 
     def issue(first, last):
         for i in range(first, min(last, len(order))):
@@ -241,11 +253,11 @@
     sent.append(head_sent)
 
     def prepare(pair):
-        loop(rows_n, lambda k: a2a_from(pair, k).wait_recv(), 1)
         lanes = lax.broadcasted_iota(jnp.int32, (LANES, LANES), 1)
-        for j in range(nz):
+
+        def take(j):
             first, second = merge(got[pair, 2 * j], got[pair, 2 * j + 1], lanes)
-            here = slice(j * LANES, (j + 1) * LANES)
+            here = pl.ds(pl.multiple_of(j * LANES, LANES), LANES)
             if pair == 1:
                 p_own[:, here] = first
             for at, value in ((0, second), (LANES, first)):
@@ -259,6 +271,18 @@
                 lhs[here, 256 + at:256 + at + LANES] = rest
                 lhs[here, 512 + at:512 + at + LANES] = high
 
+        a2a_from(pair, other).wait_recv()
+        take(z)
+
+        def arrive(i):
+            d = nz // 2 + ((i + 1) // 2) * (1 - 2 * (i % 2))
+            j = lax.rem(z + nz - d, nz)
+            a2a_from(pair, 2 * j).wait_recv()
+            a2a_from(pair, 2 * j + 1).wait_recv()
+            take(j)
+
+        loop(nz - 1, arrive)
+
     def through(stacked, count, high, rest, dot):
         both = dot(stacked, high)
         return both[:count] + both[count:] + dot(stacked[:count], rest)
@@ -273,14 +297,12 @@
     def columns(pair, j):
         here = pl.ds(pl.multiple_of(j * block, block), block)
         right = rhs[pair, :, here]
-        both = jnp.zeros((2 * slab, block), F32)
-        total = jnp.zeros((slab, block), F32)
-        for i in range(keep // block):
-            there = slice(i * block, (i + 1) * block)
+        for i in range(keep // 256):
+            there = slice(i * 256, (i + 1) * 256)
             high, rest = split(factor[there, here] * dot_nn(lhs[there, :], right))
-            both = both + dot_nn(heads[pair, :, there], high)
-            total = total + dot_nn(heads[pair, 0:slab, there], rest)
-        total = total + both[:slab] + both[slab:]
+            sym_high[there, :] = high
+            sym_rest[there, :] = rest
+        total = through(heads[pair], slab, sym_high[...], sym_rest[...], dot_nn)
         at = LANES * pair
         outer = through(low[...], slab, right[at:at + LANES], right[512 + at:512 + at + LANES], dot_nn)
         if pair == 0:
@@ -291,7 +313,7 @@
             for h in range(2):
                 for g in range(groups):
                     start = h * half + g * piece
-                    w_part[h, g * nz + j * (block // LANES) + t] = total[start:start + piece, t * LANES:(t + 1) * LANES]
+                    w_part[h, (j * (block // LANES) + t) * groups + g] = total[start:start + piece, t * LANES:(t + 1) * LANES]
 
     prepare(0)
 
@@ -317,16 +339,23 @@
 
     sent.append(head_core_sent)
 
-    for j in range(nz):
-        here = slice(j * LANES, (j + 1) * LANES)
+    def head_parts(j):
+        here = pl.ds(pl.multiple_of(j * LANES, LANES), LANES)
         head = head_all[j]
         for which, value in enumerate((head, head * values[:, here], head / values[:, here])):
             high, rest = split(value)
             heads[which, 0:slab, here] = high
             heads[which, slab:, here] = rest
 
+    loop(nz, head_parts)
     low_rank(0, 0, LANES)
     loop(keep // block, functools.partial(columns, 0))
+
+    @pl.when(jnp.logical_and(first_col, head_core))
+    def _():
+        here = pl.ds(pl.multiple_of(z * LANES, LANES), LANES)
+        w_acc[:, here] = w_acc[:, here] + head_extra[...]
+
     prepare(1)
     third[...] = low_rank(2, 1, 0)
     p_swap = remote(p_own, p_other, core_send.at[2], core_recv.at[2], (other, col))
@@ -335,33 +364,51 @@
     p_swap.start()
     third_swap.start()
     sent.extend((p_swap.wait_send, third_swap.wait_send))
-    loop(keep // block, functools.partial(columns, 1))
-
-    @pl.when(jnp.logical_and(first_col, head_core))
-    def _():
-        for h in range(2):
-            for g in range(groups):
-                start = h * half + g * piece
-                w_part[h, g * nz + z] = w_part[h, g * nz + z] + head_extra[start:start + piece, :]
-
-    w_swap = remote(w_part.at[1 - core], w_other, core_send.at[4], core_recv.at[4], (other, col))
-    w_swap.start()
-    sent.append(w_swap.wait_send)
-    w_swap.wait_recv()
-    rs_src[...] = w_part[core] + w_other[...]
-
-    def rs(k):
-        to = lax.rem(me + k, plane)
-        return remote(rs_src.at[to], rs_buf.at[me], rs_send.at[k], rs_recv.at[me], plane_device(to))
-
-    def rs_from(k):
-        source = lax.rem(me + k, plane)
-        return remote(rs_src.at[source], rs_buf.at[source], rs_send.at[k], rs_recv.at[source], plane_device(source))
-
-    loop(plane, lambda k: rs(k).start(), 1)
-    sent.append(lambda: loop(plane, lambda k: rs(k).wait_send(), 1))
+
+    per = groups * block // LANES
+
+    def w_swap(j):
+        part = pl.ds(j * per, per)
+        return remote(w_part.at[1 - core, part], w_other.at[part],
+                      core_send.at[4 + j], core_recv.at[4 + j], (other, col))
+
+    def rs(p):
+        return remote(rs_src.at[p], rs_buf.at[me], rs_send.at[p], rs_recv.at[me], plane_device(p))
+
+    def rs_from(source):
+        return remote(rs_src.at[source], rs_buf.at[source], rs_send.at[source], rs_recv.at[source],
+                      plane_device(source))
+
+    def scatter(j):
+        w_swap(j).wait_recv()
+        part = pl.ds(j * per, per)
+        rs_src[part] = w_part[core, part] + w_other[part]
+
+        def one(i):
+            p = j * per + lax.rem(me + i, per)
+
+            @pl.when(p != me)
+            def _():
+                rs(p).start()
+        loop(per, one)
+
+    def rs_sent():
+        def one(p):
+            @pl.when(p != me)
+            def _():
+                rs(p).wait_send()
+        loop(plane, one)
+
+    for j in range(keep // block):
+        columns(1, j)
+        w_swap(j).start()
+        sent.append(w_swap(j).wait_send)
+        if j:
+            scatter(j - 1)
+    scatter(keep // block - 1)
+    sent.append(rs_sent)
     rs_buf[me] = rs_src[me]
-    loop(plane, lambda k: rs_from(k).wait_recv(), 1)
+    loop(plane, lambda k: rs_from(lax.rem(me + k, plane)).wait_recv(), 1)
     ar_src[...] = jnp.sum(rs_buf[...], axis=0)
 
     def ar(k):
@@ -372,22 +419,23 @@
         source = lax.rem(across + k, nz)
         return remote(ar_src, ar_buf.at[source], ar_send.at[k], ar_recv.at[source], line_device(source))
 
-    loop(nz, lambda k: ar(k).start(), 1)
+    for d in line_order:
+        ar(d).start()
     sent.append(lambda: loop(nz, lambda k: ar(k).wait_send(), 1))
     ar_buf[across] = ar_src[...]
     loop(nz, lambda k: ar_from(k).wait_recv(), 1)
     ag_src[...] = jnp.sum(ar_buf[...], axis=0)
 
-    def ag(k):
-        to = lax.rem(me + k, plane)
-        return remote(ag_src, w_full.at[me], ag_send.at[k], ag_recv.at[me], plane_device(to))
+    def ag(to):
+        return remote(ag_src, w_full.at[me], ag_send.at[to], ag_recv.at[me], plane_device(to))
 
     def ag_from(k):
         source = lax.rem(me + k, plane)
-        return remote(ag_src, w_full.at[source], ag_send.at[k], ag_recv.at[source], plane_device(source))
-
-    loop(plane, lambda k: ag(k).start(), 1)
-    sent.append(lambda: loop(plane, lambda k: ag(k).wait_send(), 1))
+        return remote(ag_src, w_full.at[source], ag_send.at[source], ag_recv.at[source], plane_device(source))
+
+    for dx, dt in plane_order:
+        ag(around(dx, dt)).start()
+    sent.append(lambda: loop(plane, lambda k: ag(lax.rem(me + k, plane)).wait_send(), 1))
     w_full[me] = ag_src[...]
     p_swap.wait_recv()
     third_swap.wait_recv()
@@ -397,12 +445,12 @@
     theirs = jnp.zeros((half, LANES), F32)
     for j in range(nz):
         here = slice(j * LANES, (j + 1) * LANES)
-        high, rest = split(jnp.concatenate([w_full[g * nz + j] for g in range(groups)], axis=0))
+        high, rest = split(jnp.concatenate([w_full[j * groups + g] for g in range(groups)], axis=0))
         stacked = jnp.concatenate([high, rest], axis=0)
         mine = mine + through(stacked, half, rhs[1, LANES:256, here], rhs[1, 640:768, here], dot_nt)
         theirs = theirs + through(stacked, half, *split(p_other[:, here]), dot_nt)
-    mine = (mine + third[pl.ds(pl.multiple_of(core * half, 8), half), :]) * scale
-    theirs = (theirs + third_other[...]) * scale
+    mine = mine + third[pl.ds(pl.multiple_of(core * half, 8), half), :]
+    theirs = theirs + third_other[...]
     for i in range(nz):
         for at, value in ((core, mine), (1 - core, theirs)):
             out_src[i, at] = jnp.pad(value[i * out_rows:(i + 1) * out_rows], ((0, 16 - out_rows), (0, 0)))
@@ -475,19 +523,21 @@
         pltpu.VMEM((nz, piece, LANES), F32),
         pltpu.VMEM((piece, LANES), F32),
         pltpu.VMEM(pieces, F32),
+        pltpu.VMEM((keep, keep // 2), BF16),
+        pltpu.VMEM((keep, keep // 2), BF16),
         pltpu.VMEM((2 * slab, LANES), BF16),
         pltpu.VMEM((slab, LANES), F32),
         pltpu.VMEM((half, LANES), F32),
         pltpu.VMEM((nz, 2, 16, LANES), F32),
         pltpu.VMEM((nz, 2, 16, LANES), F32),
-        dma((4,)), dma((2, rows_n)), dma((2, rows_n)), dma((5,)), dma((5,)),
+        dma((4,)), dma((2, rows_n)), dma((2, rows_n)), dma((4 + keep // LANES,)), dma((4 + keep // LANES,)),
         dma((plane,)), dma((1,)), dma((nz,)), dma((nz,)), dma((plane,)), dma((plane,)),
         dma((plane,)), dma((plane,)), dma((nz,)), dma((nz,)), dma((plane,)), dma((plane,)),
         dma((nz,)), dma((nz,)),
     ]
     vmem, anywhere = pl.BlockSpec(memory_space=pltpu.VMEM), pl.BlockSpec(memory_space=pl.ANY)
     return pl.pallas_call(
-        functools.partial(kernel, (nx, ny, nz, piece, head_piece, slab, own_cols), scale),
+        functools.partial(kernel, (nx, ny, nz, piece, head_piece, slab, own_cols)),
         out_shape=jax.ShapeDtypeStruct((slab // rows_n, width), F32),
         in_specs=[anywhere] * 4 + [vmem] * 2,
         out_specs=vmem,
@@ -495,7 +545,7 @@
         compiler_params=pltpu.CompilerParams(
             collective_id=0, has_side_effects=True, vmem_limit_bytes=56 * 1024 * 1024),
         cost_estimate=pl.CostEstimate(flops=12 * 2**30, bytes_accessed=2 * 2**20, transcendentals=0),
-    )(left_vecs, left_cot, right_vecs, right_cot, values[None, :], value_cot[None, :])
+    )(left_vecs, left_cot, right_vecs, right_cot, values[None, :], value_cot[None, :]) * scale
 
 
 def build(mesh, nx, ny, nz, slab, scale):

time: 98.9 us -> 97.4 us (0.985)
  other arithmetic: 0 us -> 1.55 us
  local copies, waits for them, and re-layouts: 1.55 us -> 0 us
  Pallas kernels: 97.1 us -> 95.7 us
    mul x0 -> x1, other arithmetic: none -> 1.55 us  [body(): pl.pallas_call(functools.partial(kernel, (nx, ny, nz, piece, head_piece,...]
    unnamed x1 -> x0, local copies, waits for them, and re-layouts: 1.55 us -> none
    pallas_call x1, Pallas kernels: 97.1 us -> 95.7 us  [body(): pl.pallas_call(functools.partial(kernel, (nx, ny, nz, piece, head_piece,...]
where the time goes in v3:
time: 97.4 us; the launch traced here: 97.2 us
  Pallas kernels  95.7 us (98%)
  other arithmetic  1.55 us (2%)
    pallas_call x1, Pallas kernels, body(): pl.pallas_call(functools.partial(kernel, (nx, ny, nz, piece, head_piece,...  95.7 us

profile of v3, /device:TPU:1, one launch (start us, length us, event | category | flops | bytes accessed | tf_op | source)
XLA Modules:
  0.0 97.2 jit_solution(4465406913859456087)
XLA Ops:
  0.0 95.7 %shard_map.64 = f32[12,1664]{1,0:T(8,128)} custom-call(f32[64,1664]{1,0:T(8,128)} %refs_0_.1, f32[64,1664]{1,0:T(8,128)} %refs_1_.1, f32[64,1664]{1,0:T(8,128)} %refs_2_.1, f32[64,1664]{1,0:T(8,128)} %refs_3_.1, f32[1,1024]{1,0:T(1,128)} %bitcast.2, f32[1,1024]{1,0:T(1,128)} %bitcast.3), custom_call_target="tpu_custom_call" | custom-call | flops 12884901888 | bytes 2097152 | tf_op jit(solution)/shard_map/pallas_call | solution.py:539
  95.7 1.5 %broadcast_multiply_fusion = f32[12,1664]{1,0:T(8,128)} fusion(f32[12,1664]{1,0:T(8,128)} %shard_map.64), kind=kLoop, calls=%fused_computation | loop fusion | flops 19968 | bytes 159744 | tf_op jit(solution)/shard_map/mul | solution.py:539

commit v4 on v3

--- a/solution.py
+++ b/solution.py
@@ -41,13 +41,12 @@
     head_pieces = slab // head_piece
     groups = half // piece
     block = keep // 2
-    (a_in, b_in, p_in, q_in, values, value_cot, out,
+    (a_in, b_in, p_in, q_in, values, value_cot, out_buf,
      panels, turned, got, lhs, rhs, p_own, p_other, column, factor,
      heads, head_own, head_x, head_extra, head_slot, head_ring, head_all,
      w_acc, w_part, w_other, rs_src, rs_buf, ar_src, ar_buf, ag_src, w_full,
-     sym_high, sym_rest, low, third, third_other, out_src, out_buf,
-     load_sem, a2a_send, a2a_recv, core_send, core_recv, h1_send, h1_recv, h2_send, h2_recv,
-     h3_send, h3_recv, rs_send, rs_recv, ar_send, ar_recv, ag_send, ag_recv, o_send, o_recv) = refs
+     sym_high, sym_rest, low, third, third_other, last_left, last_high, last_rest, out_src,
+     load_sem, a2a_send, a2a_recv, core_send, core_recv, head_send, head_recv, sum_send, sum_recv, own_sem) = refs
 
     row = lax.axis_index("row")
     col = lax.axis_index("col")
@@ -110,35 +109,32 @@
     for d, c in row_order:
         greet((row_target(d, c), col))
 
-    loads = [
-        pltpu.make_async_copy(source, panels.at[i // 2, pl.ds(64 * (i % 2), 64)], load_sem.at[i])
-        for i, source in enumerate((a_in, b_in, p_in, q_in))
-    ]
-    for copy in loads:
-        copy.start()
-    got[:, :, own_cols:, :] = jnp.zeros((2, rows_n, LANES - own_cols, LANES), F32)
+    for i, source in enumerate((a_in, b_in, p_in, q_in)):
+        pltpu.make_async_copy(source, panels.at[i // 2, pl.ds(64 * (i % 2), 64)], load_sem.at[i // 2]).start()
 
     def turn(pair):
-        loads[2 * pair].wait()
-        loads[2 * pair + 1].wait()
+        pltpu.make_async_copy(panels.at[pair], panels.at[pair], load_sem.at[pair]).wait()
         for tile in range(width // LANES):
             turned[pair, tile * LANES:(tile + 1) * LANES, :] = panels[pair, :, tile * LANES:(tile + 1) * LANES].T
 
     turn(0)
-    turn(1)
     pl.semaphore_wait(barrier, rows_n - 1 + plane - 1 + nz - 1)
 
-    def a2a(pair, d, c):
+    def arrival(pair, chip):
+        return a2a_recv.at[0 if pair == 0 else 1 + chip]
+
+    def a2a(pair, d, c, send):
         to = row_target(d, c)
         return remote(
             turned.at[pair, pl.ds(pl.multiple_of(to * own_cols, 8), own_cols)],
             got.at[pair, row, pl.ds(0, own_cols)],
-            a2a_send.at[pair, 2 * d + c], a2a_recv.at[pair, row], (to, col))
-
-    def a2a_from(pair, source):
-        return remote(
-            turned.at[pair, pl.ds(0, own_cols)], got.at[pair, source, pl.ds(0, own_cols)],
-            a2a_send.at[pair, 0], a2a_recv.at[pair, source], (source, col))
+            a2a_send.at[send], arrival(pair, z), (to, col))
+
+    def landed(ref, semaphore):
+        remote(ref, ref, core_send.at[0], semaphore, (other, col)).wait_recv()
+
+    def left(ref, semaphore):
+        remote(ref, ref, semaphore, core_recv.at[0], (other, col)).wait_send()
 
     first_col = col == 0
     head_core = core == 0
@@ -153,24 +149,15 @@
 
     def h1(p):
         return remote(head_own.at[pl.ds(pl.multiple_of(p * head_piece, 8), head_piece)], head_slot,
-                      h1_send.at[p], h1_recv.at[0], (row, p))
-
-    def h2(k):
-        to = lax.rem(z + k, nz)
-        return remote(head_slot, head_ring.at[z], h2_send.at[k], h2_recv.at[z], (to * 2 + core, col))
-
-    def h2_from(k):
-        source = lax.rem(z + k, nz)
-        return remote(head_slot, head_ring.at[source], h2_send.at[k], h2_recv.at[source], (source * 2 + core, col))
-
-    def head_rows(p):
-        return head_all.at[:, pl.ds(pl.multiple_of(p * head_piece, 8), head_piece)]
+                      head_send.at[0], head_recv.at[0], (row, p))
+
+    def h2(d):
+        return remote(head_slot, head_ring.at[z], head_send.at[1], head_recv.at[1],
+                      (lax.rem(z + d, nz) * 2 + core, col))
 
     def h3(k):
-        return remote(head_ring, head_rows(col), h3_send.at[k], h3_recv.at[col], (row, lax.rem(col + k, plane)))
-
-    def h3_from(p):
-        return remote(head_ring, head_rows(p), h3_send.at[0], h3_recv.at[p], (row, p))
+        return remote(head_ring, head_all.at[:, pl.ds(pl.multiple_of(col * head_piece, 8), head_piece)],
+                      head_send.at[2], head_recv.at[2], (row, lax.rem(col + k, plane)))
 
     order = [(pair, d, c) for pair in range(2) for d, c in row_order]
     window = min(6, len(row_order) // 2)
@@ -178,8 +165,8 @@
     def issue(first, last):
         for i in range(first, min(last, len(order))):
             if window <= i < 2 * window:
-                a2a(*order[i - window]).wait_send()
-            a2a(*order[i]).start()
+                left(turned.at[0, pl.ds(0, own_cols)], a2a_send.at[i - window])
+            a2a(*order[i], i if i < window else window + order[i][0]).start()
 
     @pl.when(jnp.logical_and(first_col, core == 1))
     def _():
@@ -201,6 +188,8 @@
     def _():
         to_core0.wait_send()
 
+    turn(1)
+    got[:, :, own_cols:, :] = jnp.zeros((2, rows_n, LANES - own_cols, LANES), F32)
     for pair in range(2):
         got[pair, row, 0:own_cols, :] = turned[pair, pl.ds(pl.multiple_of(row * own_cols, 8), own_cols), :]
 
@@ -208,23 +197,24 @@
     def _():
         @pl.when(jnp.logical_not(first_col))
         def _():
-            h1(col).wait_recv()
-        loop(nz, lambda k: h2(k).start(), 1)
+            landed(head_slot, head_recv.at[0])
+        for d in line_order:
+            h2(d).start()
         head_ring[z] = head_slot[...]
 
     issue(window, 2 * window)
 
     @pl.when(carries)
     def _():
-        loop(nz, lambda k: h2_from(k).wait_recv(), 1)
+        landed(head_ring.at[pl.ds(0, nz - 1)], head_recv.at[1])
         loop(plane, lambda k: h3(k).start(), 1)
         head_all[:, pl.ds(pl.multiple_of(col * head_piece, 8), head_piece), :] = head_ring[...]
 
     issue(2 * window, len(order))
 
     def a2a_sent():
-        for item in order[window:]:
-            a2a(*item).wait_send()
+        left(turned.at[0, pl.ds(0, (len(row_order) - window) * own_cols)], a2a_send.at[window])
+        left(turned.at[1, pl.ds(0, len(row_order) * own_cols)], a2a_send.at[window + 1])
 
     sent.append(a2a_sent)
 
@@ -243,14 +233,18 @@
     def head_sent():
         @pl.when(jnp.logical_and(first_col, head_core))
         def _():
-            loop(head_pieces, lambda p: h1(p).wait_send(), 1)
+            left(head_own.at[pl.ds(0, slab - head_piece)], head_send.at[0])
 
         @pl.when(carries)
         def _():
-            loop(nz, lambda k: h2(k).wait_send(), 1)
-            loop(plane, lambda k: h3(k).wait_send(), 1)
+            left(head_ring.at[pl.ds(0, nz - 1)], head_send.at[1])
+            left(factor.at[pl.ds(0, (plane - 1) * head_piece)], head_send.at[2])
 
     sent.append(head_sent)
+
+    def through(stacked, count, high, rest, dot):
+        both = dot(stacked, high)
+        return both[:count] + both[count:] + dot(stacked[:count], rest)
 
     def prepare(pair):
         lanes = lax.broadcasted_iota(jnp.int32, (LANES, LANES), 1)
@@ -265,34 +259,32 @@
                 rhs[pair, at:at + LANES, here] = high
                 rhs[pair, 256 + at:256 + at + LANES, here] = high
                 rhs[pair, 512 + at:512 + at + LANES, here] = rest
+                if pair == 1 and at == 0:
+                    third[...] = third[...] + through(heads[2, :, here], slab, high, rest, dot_nt)
             for at, value in ((0, first.T), (LANES, -second.T)):
                 high, rest = split(value)
                 lhs[here, at:at + LANES] = high
                 lhs[here, 256 + at:256 + at + LANES] = rest
                 lhs[here, 512 + at:512 + at + LANES] = high
 
-        a2a_from(pair, other).wait_recv()
-        take(z)
-
         def arrive(i):
             d = nz // 2 + ((i + 1) // 2) * (1 - 2 * (i % 2))
             j = lax.rem(z + nz - d, nz)
-            a2a_from(pair, 2 * j).wait_recv()
-            a2a_from(pair, 2 * j + 1).wait_recv()
+            if pair == 1:
+                landed(got.at[pair, pl.ds(2 * j, 2), pl.ds(0, own_cols)], arrival(pair, j))
             take(j)
 
+        if pair == 0:
+            landed(got.at[pair, pl.ds(0, rows_n - 1), pl.ds(0, own_cols)], arrival(pair, z))
+        else:
+            landed(got.at[pair, 0, pl.ds(0, own_cols)], arrival(pair, z))
+        take(z)
         loop(nz - 1, arrive)
 
-    def through(stacked, count, high, rest, dot):
-        both = dot(stacked, high)
-        return both[:count] + both[count:] + dot(stacked[:count], rest)
-
-    def low_rank(which, pair, at):
-        value = through(heads[which], slab, rhs[pair, at:at + LANES, :], rhs[pair, 512 + at:512 + at + LANES, :], dot_nt)
+    def set_low(value):
         high, rest = split(value)
         low[0:slab, :] = high
         low[slab:, :] = rest
-        return value
 
     def columns(pair, j):
         here = pl.ds(pl.multiple_of(j * block, block), block)
@@ -321,11 +313,13 @@
 
     @pl.when(head_core)
     def _():
-        def arrived(p):
-            @pl.when(p != col)
-            def _():
-                h3_from(p).wait_recv()
-        loop(head_pieces, arrived)
+        @pl.when(col < head_pieces)
+        def _():
+            landed(head_all.at[:, pl.ds(0, slab - head_piece)], head_recv.at[2])
+
+        @pl.when(col >= head_pieces)
+        def _():
+            landed(head_all, head_recv.at[2])
         to_core1.start()
 
     @pl.when(core == 1)
@@ -348,7 +342,7 @@
             heads[which, slab:, here] = rest
 
     loop(nz, head_parts)
-    low_rank(0, 0, LANES)
+    set_low(through(heads[0], slab, rhs[0, LANES:256, :], rhs[0, 640:768, :], dot_nt))
     loop(keep // block, functools.partial(columns, 0))
 
     @pl.when(jnp.logical_and(first_col, head_core))
@@ -356,8 +350,9 @@
         here = pl.ds(pl.multiple_of(z * LANES, LANES), LANES)
         w_acc[:, here] = w_acc[:, here] + head_extra[...]
 
+    third[...] = jnp.zeros((slab, LANES), F32)
     prepare(1)
-    third[...] = low_rank(2, 1, 0)
+    set_low(third[...])
     p_swap = remote(p_own, p_other, core_send.at[2], core_recv.at[2], (other, col))
     third_swap = remote(third.at[pl.ds(pl.multiple_of((1 - core) * half, 8), half)], third_other,
                         core_send.at[3], core_recv.at[3], (other, col))
@@ -372,12 +367,14 @@
         return remote(w_part.at[1 - core, part], w_other.at[part],
                       core_send.at[4 + j], core_recv.at[4 + j], (other, col))
 
-    def rs(p):
-        return remote(rs_src.at[p], rs_buf.at[me], rs_send.at[p], rs_recv.at[me], plane_device(p))
-
-    def rs_from(source):
-        return remote(rs_src.at[source], rs_buf.at[source], rs_send.at[source], rs_recv.at[source],
-                      plane_device(source))
+    mine_now = (lax.rem(along, 2) * (nz // 2) + along // 2) * groups + x
+
+    def owner(q):
+        zb, g = q // groups, q % groups
+        return g * ny + 2 * (zb % (nz // 2)) + zb // (nz // 2)
+
+    def rs(q):
+        return remote(rs_src.at[q], rs_buf.at[me], sum_send.at[0], sum_recv.at[0], plane_device(owner(q)))
 
     def scatter(j):
         w_swap(j).wait_recv()
@@ -385,19 +382,12 @@
         rs_src[part] = w_part[core, part] + w_other[part]
 
         def one(i):
-            p = j * per + lax.rem(me + i, per)
-
-            @pl.when(p != me)
+            q = j * per + lax.rem(me + i, per)
+
+            @pl.when(q != mine_now)
             def _():
-                rs(p).start()
+                rs(q).start()
         loop(per, one)
-
-    def rs_sent():
-        def one(p):
-            @pl.when(p != me)
-            def _():
-                rs(p).wait_send()
-        loop(plane, one)
 
     for j in range(keep // block):
         columns(1, j)
@@ -406,88 +396,78 @@
         if j:
             scatter(j - 1)
     scatter(keep // block - 1)
-    sent.append(rs_sent)
-    rs_buf[me] = rs_src[me]
-    loop(plane, lambda k: rs_from(lax.rem(me + k, plane)).wait_recv(), 1)
+    sent.append(lambda: left(rs_buf.at[pl.ds(0, plane - 1)], sum_send.at[0]))
+    rs_buf[me] = rs_src[mine_now]
+    landed(rs_buf.at[pl.ds(0, plane - 1)], sum_recv.at[0])
     ar_src[...] = jnp.sum(rs_buf[...], axis=0)
 
-    def ar(k):
-        to = lax.rem(across + k, nz)
-        return remote(ar_src, ar_buf.at[across], ar_send.at[k], ar_recv.at[across], line_device(to))
-
-    def ar_from(k):
-        source = lax.rem(across + k, nz)
-        return remote(ar_src, ar_buf.at[source], ar_send.at[k], ar_recv.at[source], line_device(source))
-
     for d in line_order:
-        ar(d).start()
-    sent.append(lambda: loop(nz, lambda k: ar(k).wait_send(), 1))
+        remote(ar_src, ar_buf.at[across], sum_send.at[1], sum_recv.at[1],
+               line_device(lax.rem(across + d, nz))).start()
+    sent.append(lambda: left(ar_buf.at[pl.ds(0, nz - 1)], sum_send.at[1]))
     ar_buf[across] = ar_src[...]
-    loop(nz, lambda k: ar_from(k).wait_recv(), 1)
+    landed(ar_buf.at[pl.ds(0, nz - 1)], sum_recv.at[1])
     ag_src[...] = jnp.sum(ar_buf[...], axis=0)
 
-    def ag(to):
-        return remote(ag_src, w_full.at[me], ag_send.at[to], ag_recv.at[me], plane_device(to))
-
-    def ag_from(k):
-        source = lax.rem(me + k, plane)
-        return remote(ag_src, w_full.at[source], ag_send.at[source], ag_recv.at[source], plane_device(source))
-
     for dx, dt in plane_order:
-        ag(around(dx, dt)).start()
-    sent.append(lambda: loop(plane, lambda k: ag(lax.rem(me + k, plane)).wait_send(), 1))
+        remote(ag_src, w_full.at[me], sum_send.at[2], sum_recv.at[2], plane_device(around(dx, dt))).start()
+    sent.append(lambda: left(w_full.at[pl.ds(0, plane - 1)], sum_send.at[2]))
     w_full[me] = ag_src[...]
     p_swap.wait_recv()
     third_swap.wait_recv()
-    loop(plane, lambda k: ag_from(k).wait_recv(), 1)
-
-    mine = jnp.zeros((half, LANES), F32)
-    theirs = jnp.zeros((half, LANES), F32)
-    for j in range(nz):
-        here = slice(j * LANES, (j + 1) * LANES)
-        high, rest = split(jnp.concatenate([w_full[j * groups + g] for g in range(groups)], axis=0))
-        stacked = jnp.concatenate([high, rest], axis=0)
-        mine = mine + through(stacked, half, rhs[1, LANES:256, here], rhs[1, 640:768, here], dot_nt)
-        theirs = theirs + through(stacked, half, *split(p_other[:, here]), dot_nt)
-    mine = mine + third[pl.ds(pl.multiple_of(core * half, 8), half), :]
-    theirs = theirs + third_other[...]
+    last_high[0:LANES, :] = rhs[1, LANES:256, :]
+    last_rest[0:LANES, :] = rhs[1, 640:768, :]
+    high, rest = split(p_other[...])
+    last_high[LANES:, :] = high
+    last_rest[LANES:, :] = rest
+    landed(w_full.at[pl.ds(0, plane - 1)], sum_recv.at[2])
+
+    for zb in range(nz):
+        here = slice(zb * LANES, (zb + 1) * LANES)
+        t = 2 * (zb % (nz // 2)) + zb // (nz // 2)
+        high, rest = split(jnp.concatenate([w_full[g * ny + t] for g in range(groups)], axis=0))
+        last_left[0:half, here] = high
+        last_left[half:, here] = rest
+    product = through(last_left[...], half, last_high[...], last_rest[...], dot_nt)
+    mine = product[:, :LANES] + third[pl.ds(pl.multiple_of(core * half, 8), half), :]
+    theirs = product[:, LANES:] + third_other[...]
     for i in range(nz):
         for at, value in ((core, mine), (1 - core, theirs)):
-            out_src[i, at] = jnp.pad(value[i * out_rows:(i + 1) * out_rows], ((0, 16 - out_rows), (0, 0)))
+            out_src[i, at] = value[i * out_rows:(i + 1) * out_rows]
 
     def send_out(i):
-        to = core * nz + i
-        return remote(out_src.at[i], out_buf.at[z], o_send.at[i], o_recv.at[z], (to, col))
-
-    def out_from(i):
-        source = 2 * i + row // nz
-        return remote(out_src.at[i], out_buf.at[i], o_send.at[i], o_recv.at[i], (source, col))
-
-    def each_out(step):
-        def run(i):
-            @pl.when(core * nz + i != row)
-            def _():
-                step(send_out(i))
-        loop(nz, run)
-
-    each_out(lambda copy: copy.start())
-
-    @pl.when(core == row // nz)
-    def _():
-        out_buf[z] = out_src[lax.rem(row, nz)]
-
-    def out_arrived(i):
-        @pl.when(2 * i + row // nz != row)
-        def _():
-            out_from(i).wait_recv()
-    loop(nz, out_arrived)
-    for i in range(nz):
+        return remote(out_src.at[i], out_buf.at[z], sum_send.at[3], sum_recv.at[3], (core * nz + i, col))
+
+    for d in range(nz):
+        i = lax.rem(z + d + nz // 2, nz)
+
+        @pl.when(core * nz + i != row)
+        def _():
+            send_out(i).start()
+
+    keeps = core == row // nz
+    own_out = pltpu.make_async_copy(out_src.at[lax.rem(row, nz)], out_buf.at[z], own_sem.at[0])
+
+    @pl.when(keeps)
+    def _():
+        own_out.start()
+        landed(out_buf.at[pl.ds(0, nz - 1)], sum_recv.at[3])
+        left(out_src.at[pl.ds(0, nz - 1)], sum_send.at[3])
+        own_out.wait()
+
+    @pl.when(jnp.logical_not(keeps))
+    def _():
+        landed(out_buf, sum_recv.at[3])
+        left(out_src, sum_send.at[3])
+
+    settle()
+
+
+def lay_out(own_cols, scale, blocks, out):
+    for i in range(blocks.shape[0]):
         for c in range(2):
             start = (2 * i + c) * own_cols
-            out[:, start:start + own_cols] = out_buf[i, c, 0:out_rows, 0:own_cols]
-
-    each_out(lambda copy: copy.wait_send())
-    settle()
+            out[:, start:start + own_cols] = blocks[i, c, :, 0:own_cols] * scale
 
 
 def body(nx, ny, nz, slab, scale, left_vecs, left_cot, right_vecs, right_cot, values, value_cot):
@@ -528,24 +508,29 @@
         pltpu.VMEM((2 * slab, LANES), BF16),
         pltpu.VMEM((slab, LANES), F32),
         pltpu.VMEM((half, LANES), F32),
-        pltpu.VMEM((nz, 2, 16, LANES), F32),
-        pltpu.VMEM((nz, 2, 16, LANES), F32),
-        dma((4,)), dma((2, rows_n)), dma((2, rows_n)), dma((4 + keep // LANES,)), dma((4 + keep // LANES,)),
-        dma((plane,)), dma((1,)), dma((nz,)), dma((nz,)), dma((plane,)), dma((plane,)),
-        dma((plane,)), dma((plane,)), dma((nz,)), dma((nz,)), dma((plane,)), dma((plane,)),
-        dma((nz,)), dma((nz,)),
+        pltpu.VMEM((2 * half, keep), BF16),
+        pltpu.VMEM((2 * LANES, keep), BF16),
+        pltpu.VMEM((2 * LANES, keep), BF16),
+        pltpu.VMEM((nz, 2, slab // rows_n, LANES), F32),
+        dma((2,)), dma((8,)), dma((1 + nz,)), dma((6,)), dma((6,)), dma((3,)), dma((3,)),
+        dma((4,)), dma((4,)), dma((1,)),
     ]
     vmem, anywhere = pl.BlockSpec(memory_space=pltpu.VMEM), pl.BlockSpec(memory_space=pl.ANY)
-    return pl.pallas_call(
+    blocks = pl.pallas_call(
         functools.partial(kernel, (nx, ny, nz, piece, head_piece, slab, own_cols)),
-        out_shape=jax.ShapeDtypeStruct((slab // rows_n, width), F32),
+        out_shape=jax.ShapeDtypeStruct((nz, 2, slab // rows_n, LANES), F32),
         in_specs=[anywhere] * 4 + [vmem] * 2,
-        out_specs=vmem,
+        out_specs=anywhere,
         scratch_shapes=scratch,
         compiler_params=pltpu.CompilerParams(
             collective_id=0, has_side_effects=True, vmem_limit_bytes=56 * 1024 * 1024),
         cost_estimate=pl.CostEstimate(flops=12 * 2**30, bytes_accessed=2 * 2**20, transcendentals=0),
-    )(left_vecs, left_cot, right_vecs, right_cot, values[None, :], value_cot[None, :]) * scale
+    )(left_vecs, left_cot, right_vecs, right_cot, values[None, :], value_cot[None, :])
+    return pl.pallas_call(
+        functools.partial(lay_out, own_cols, scale),
+        out_shape=jax.ShapeDtypeStruct((slab // rows_n, width), F32),
+        in_specs=[vmem], out_specs=vmem,
+    )(blocks)
 
 
 def build(mesh, nx, ny, nz, slab, scale):

time: 97.4 us -> 90.9 us (0.933)
  Pallas kernels: 95.7 us -> 90.7 us
  other arithmetic: 1.55 us -> 0 us
    pallas_call x1, Pallas kernels: 95.7 us -> 89.1 us  [body(): pl.pallas_call(functools.partial(kernel, (nx, ny, nz, piece, head_piece,...]
    pallas_call x0 -> x1, Pallas kernels: none -> 1.65 us  [body(): pl.pallas_call(functools.partial(lay_out, own_cols, scale), out_shape=jax...]
    mul x1 -> x0, other arithmetic: 1.55 us -> none  [body(): pl.pallas_call(functools.partial(kernel, (nx, ny, nz, piece, head_piece,...]
where the time goes in v4:
time: 90.9 us; the launch traced here: 90.7 us
  Pallas kernels  90.7 us (100%)
    pallas_call x1, Pallas kernels, body(): pl.pallas_call(functools.partial(kernel, (nx, ny, nz, piece, head_piece,...  89.1 us

profile of v4, /device:TPU:1, one launch (start us, length us, event | category | flops | bytes accessed | tf_op | source)
XLA Modules:
  0.0 90.7 jit_solution(702394640009435011)
XLA Ops:
  0.0 89.1 %shard_map.64.blocks = f32[8,2,12,128]{3,2,1,0:T(8,128)} custom-call(f32[64,1664]{1,0:T(8,128)} %refs_0_.1, f32[64,1664]{1,0:T(8,128)} %refs_1_.1, f32[64,1664]{1,0:T(8,128)} %refs_2_.1, f32[64,1664]{1,0:T(8,128)} %refs_3_.1, f32[1,1024]{1,0:T(1,128)} %bitcast.2, f32[1,1024]{1,0:T(1,128)} %bitcast.3), custom_call_target="tpu_custom_call" | custom-call | flops 12884901888 | bytes 2097152 | tf_op jit(solution)/shard_map/pallas_call | solution.py:519
  89.1 1.6 %shard_map.65 = f32[12,1664]{1,0:T(8,128)} custom-call(f32[8,2,12,128]{3,2,1,0:T(8,128)} %shard_map.64.blocks), custom_call_target="tpu_custom_call" | custom-call | tf_op jit(solution)/shard_map/pallas_call | solution.py:529

commit v5 on v4

--- a/solution.py
+++ b/solution.py
@@ -102,15 +102,15 @@
     def greet(device):
         pl.semaphore_signal(barrier, inc=1, device_id=device, device_id_type=pl.DeviceIdType.MESH)
 
+    for i, source in enumerate((a_in, b_in, p_in, q_in)):
+        pltpu.make_async_copy(source, panels.at[i // 2, pl.ds(64 * (i % 2), 64)], load_sem.at[i // 2]).start()
+
     for dx, dt in plane_order:
         greet(plane_device(around(dx, dt)))
     for d in line_order:
         greet(line_device(lax.rem(across + d, nz)))
     for d, c in row_order:
         greet((row_target(d, c), col))
-
-    for i, source in enumerate((a_in, b_in, p_in, q_in)):
-        pltpu.make_async_copy(source, panels.at[i // 2, pl.ds(64 * (i % 2), 64)], load_sem.at[i // 2]).start()
 
     def turn(pair):
         pltpu.make_async_copy(panels.at[pair], panels.at[pair], load_sem.at[pair]).wait()
@@ -287,14 +287,16 @@
         low[slab:, :] = rest
 
     def columns(pair, j):
-        here = pl.ds(pl.multiple_of(j * block, block), block)
+        here = slice(j * block, (j + 1) * block)
         right = rhs[pair, :, here]
-        for i in range(keep // 256):
-            there = slice(i * 256, (i + 1) * 256)
-            high, rest = split(factor[there, here] * dot_nn(lhs[there, :], right))
-            sym_high[there, :] = high
-            sym_rest[there, :] = rest
-        total = through(heads[pair], slab, sym_high[...], sym_rest[...], dot_nn)
+        step = min(256, block)
+        for start in range(block * j, keep, step):
+            there = slice(start, start + step)
+            value = factor[there, here] * dot_nn(lhs[there, :], right)
+            sym_high[there, here], sym_rest[there, here] = split(value)
+            if start >= block * (j + 1):
+                sym_high[here, there], sym_rest[here, there] = split(value.T)
+        total = through(heads[pair], slab, sym_high[:, here], sym_rest[:, here], dot_nn)
         at = LANES * pair
         outer = through(low[...], slab, right[at:at + LANES], right[512 + at:512 + at + LANES], dot_nn)
         if pair == 0:
@@ -343,7 +345,8 @@
 
     loop(nz, head_parts)
     set_low(through(heads[0], slab, rhs[0, LANES:256, :], rhs[0, 640:768, :], dot_nt))
-    loop(keep // block, functools.partial(columns, 0))
+    for j in range(keep // block):
+        columns(0, j)
 
     @pl.when(jnp.logical_and(first_col, head_core))
     def _():
@@ -369,25 +372,28 @@
 
     mine_now = (lax.rem(along, 2) * (nz // 2) + along // 2) * groups + x
 
-    def owner(q):
-        zb, g = q // groups, q % groups
-        return g * ny + 2 * (zb % (nz // 2)) + zb // (nz // 2)
-
-    def rs(q):
-        return remote(rs_src.at[q], rs_buf.at[me], sum_send.at[0], sum_recv.at[0], plane_device(owner(q)))
+    def rs(j, dx, i):
+        t = lax.rem(along + i * 2 + lax.rem(along + j, 2), ny)
+        g = lax.rem(x + dx, nx)
+        q = (lax.rem(t, 2) * (nz // 2) + t // 2) * groups + g
+        return remote(rs_src.at[q], rs_buf.at[me], sum_send.at[0], sum_recv.at[0], plane_device(g * ny + t))
+
+    rs_order = sorted(
+        ((dx, i) for dx in range(nx) for i in range(ny // 2)),
+        key=lambda at: -min(at[0], nx - at[0]) - abs(ny / 2 - abs(2 * at[1] + 0.5 - ny / 2)))
 
     def scatter(j):
         w_swap(j).wait_recv()
         part = pl.ds(j * per, per)
         rs_src[part] = w_part[core, part] + w_other[part]
 
-        def one(i):
-            q = j * per + lax.rem(me + i, per)
-
-            @pl.when(q != mine_now)
-            def _():
-                rs(q).start()
-        loop(per, one)
+        for dx, i in rs_order:
+            if dx or i:
+                rs(j, dx, i).start()
+            else:
+                @pl.when(lax.rem(along + j, 2) == 1)
+                def _():
+                    rs(j, dx, i).start()
 
     for j in range(keep // block):
         columns(1, j)
@@ -410,7 +416,7 @@
     ag_src[...] = jnp.sum(ar_buf[...], axis=0)
 
     for dx, dt in plane_order:
-        remote(ag_src, w_full.at[me], sum_send.at[2], sum_recv.at[2], plane_device(around(dx, dt))).start()
+        remote(ag_src, w_full.at[me], sum_send.at[2], sum_recv.at[4 + x], plane_device(around(dx, dt))).start()
     sent.append(lambda: left(w_full.at[pl.ds(0, plane - 1)], sum_send.at[2]))
     w_full[me] = ag_src[...]
     p_swap.wait_recv()
@@ -420,30 +426,43 @@
     high, rest = split(p_other[...])
     last_high[LANES:, :] = high
     last_rest[LANES:, :] = rest
-    landed(w_full.at[pl.ds(0, plane - 1)], sum_recv.at[2])
-
-    for zb in range(nz):
-        here = slice(zb * LANES, (zb + 1) * LANES)
-        t = 2 * (zb % (nz // 2)) + zb // (nz // 2)
-        high, rest = split(jnp.concatenate([w_full[g * ny + t] for g in range(groups)], axis=0))
-        last_left[0:half, here] = high
-        last_left[half:, here] = rest
-    product = through(last_left[...], half, last_high[...], last_rest[...], dot_nt)
-    mine = product[:, :LANES] + third[pl.ds(pl.multiple_of(core * half, 8), half), :]
-    theirs = product[:, LANES:] + third_other[...]
-    for i in range(nz):
-        for at, value in ((core, mine), (1 - core, theirs)):
-            out_src[i, at] = value[i * out_rows:(i + 1) * out_rows]
+    last_left[...] = jnp.zeros(last_left.shape, BF16)
 
     def send_out(i):
         return remote(out_src.at[i], out_buf.at[z], sum_send.at[3], sum_recv.at[3], (core * nz + i, col))
 
-    for d in range(nz):
-        i = lax.rem(z + d + nz // 2, nz)
-
-        @pl.when(core * nz + i != row)
-        def _():
-            send_out(i).start()
+    def finish(i):
+        dx = i + (i // 2) * (1 - 2 * (i % 2))
+        g = lax.rem(x + dx, nx)
+
+        @pl.when(dx == 0)
+        def _():
+            landed(w_full.at[pl.ds(0, ny - 1)], sum_recv.at[4 + g])
+
+        @pl.when(dx != 0)
+        def _():
+            landed(w_full.at[pl.ds(0, ny)], sum_recv.at[4 + g])
+
+        for zb in range(nz):
+            here = slice(zb * LANES, (zb + 1) * LANES)
+            high, rest = split(w_full[g * ny + 2 * (zb % (nz // 2)) + zb // (nz // 2)])
+            last_left[0:piece, here] = high
+            last_left[32:32 + piece, here] = rest
+        both = dot_nt(last_left[...], last_high[...])
+        product = both[0:piece] + both[32:32 + piece] + dot_nt(last_left[0:32, :], last_rest[...])[0:piece]
+        mine = product[:, :LANES] + third[pl.ds(pl.multiple_of(core * half + g * piece, 8), piece), :]
+        theirs = product[:, LANES:] + third_other[pl.ds(pl.multiple_of(g * piece, 8), piece), :]
+        for c in range(2):
+            to = 2 * g + c
+            rows = slice(c * out_rows, (c + 1) * out_rows)
+            out_src[to, core] = mine[rows]
+            out_src[to, 1 - core] = theirs[rows]
+
+            @pl.when(core * nz + to != row)
+            def _():
+                send_out(to).start()
+
+    loop(nx, finish)
 
     keeps = core == row // nz
     own_out = pltpu.make_async_copy(out_src.at[lax.rem(row, nz)], out_buf.at[z], own_sem.at[0])
@@ -503,17 +522,17 @@
         pltpu.VMEM((nz, piece, LANES), F32),
         pltpu.VMEM((piece, LANES), F32),
         pltpu.VMEM(pieces, F32),
-        pltpu.VMEM((keep, keep // 2), BF16),
-        pltpu.VMEM((keep, keep // 2), BF16),
+        pltpu.VMEM((keep, keep), BF16),
+        pltpu.VMEM((keep, keep), BF16),
         pltpu.VMEM((2 * slab, LANES), BF16),
         pltpu.VMEM((slab, LANES), F32),
         pltpu.VMEM((half, LANES), F32),
-        pltpu.VMEM((2 * half, keep), BF16),
+        pltpu.VMEM((64, keep), BF16),
         pltpu.VMEM((2 * LANES, keep), BF16),
         pltpu.VMEM((2 * LANES, keep), BF16),
         pltpu.VMEM((nz, 2, slab // rows_n, LANES), F32),
         dma((2,)), dma((8,)), dma((1 + nz,)), dma((6,)), dma((6,)), dma((3,)), dma((3,)),
-        dma((4,)), dma((4,)), dma((1,)),
+        dma((4,)), dma((4 + nx,)), dma((1,)),
     ]
     vmem, anywhere = pl.BlockSpec(memory_space=pltpu.VMEM), pl.BlockSpec(memory_space=pl.ANY)
     blocks = pl.pallas_call(

time: 90.9 us -> 88.6 us (0.975)
  Pallas kernels: 90.7 us -> 88.5 us
    pallas_call x1, Pallas kernels: 89.1 us -> 86.8 us  [body(): pl.pallas_call(functools.partial(kernel, (nx, ny, nz, piece, head_piece,...]
where the time goes in v5:
time: 88.6 us; the launch traced here: 88.5 us
  Pallas kernels  88.5 us (100%)
    pallas_call x1, Pallas kernels, body(): pl.pallas_call(functools.partial(kernel, (nx, ny, nz, piece, head_piece,...  86.8 us

profile of v5, /device:TPU:1, one launch (start us, length us, event | category | flops | bytes accessed | tf_op | source)
XLA Modules:
  0.0 88.5 jit_solution(1791308797386550991)
XLA Ops:
  0.0 86.8 %shard_map.64.blocks = f32[8,2,12,128]{3,2,1,0:T(8,128)} custom-call(f32[64,1664]{1,0:T(8,128)} %refs_0_.1, f32[64,1664]{1,0:T(8,128)} %refs_1_.1, f32[64,1664]{1,0:T(8,128)} %refs_2_.1, f32[64,1664]{1,0:T(8,128)} %refs_3_.1, f32[1,1024]{1,0:T(1,128)} %bitcast.2, f32[1,1024]{1,0:T(1,128)} %bitcast.3), custom_call_target="tpu_custom_call" | custom-call | flops 12884901888 | bytes 2097152 | tf_op jit(solution)/shard_map/pallas_call | solution.py:538
  86.8 1.6 %shard_map.65 = f32[12,1664]{1,0:T(8,128)} custom-call(f32[8,2,12,128]{3,2,1,0:T(8,128)} %shard_map.64.blocks), custom_call_target="tpu_custom_call" | custom-call | tf_op jit(solution)/shard_map/pallas_call | solution.py:548

commit v6 on v5

--- a/solution.py
+++ b/solution.py
@@ -46,7 +46,7 @@
      heads, head_own, head_x, head_extra, head_slot, head_ring, head_all,
      w_acc, w_part, w_other, rs_src, rs_buf, ar_src, ar_buf, ag_src, w_full,
      sym_high, sym_rest, low, third, third_other, last_left, last_high, last_rest, out_src,
-     load_sem, a2a_send, a2a_recv, core_send, core_recv, head_send, head_recv, sum_send, sum_recv, own_sem) = refs
+     load_sem, a2a_send, a2a_recv, core_send, core_recv, head_send, head_recv, sum_send, sum_recv, own_sem, known) = refs
 
     row = lax.axis_index("row")
     col = lax.axis_index("col")
@@ -105,12 +105,12 @@
     for i, source in enumerate((a_in, b_in, p_in, q_in)):
         pltpu.make_async_copy(source, panels.at[i // 2, pl.ds(64 * (i % 2), 64)], load_sem.at[i // 2]).start()
 
-    for dx, dt in plane_order:
-        greet(plane_device(around(dx, dt)))
+    for d, c in row_order[1:] + row_order[:1]:
+        greet((row_target(d, c), col))
     for d in line_order:
-        greet(line_device(lax.rem(across + d, nz)))
-    for d, c in row_order:
-        greet((row_target(d, c), col))
+        greet((row, x * ny + lax.rem(y + d, ny)))
+    for d in range(1, nx):
+        greet((row, lax.rem(x + d, nx) * ny + y))
 
     def turn(pair):
         pltpu.make_async_copy(panels.at[pair], panels.at[pair], load_sem.at[pair]).wait()
@@ -118,7 +118,7 @@
             turned[pair, tile * LANES:(tile + 1) * LANES, :] = panels[pair, :, tile * LANES:(tile + 1) * LANES].T
 
     turn(0)
-    pl.semaphore_wait(barrier, rows_n - 1 + plane - 1 + nz - 1)
+    pl.semaphore_wait(barrier, rows_n - 1 + ny - 1 + nx - 1)
 
     def arrival(pair, chip):
         return a2a_recv.at[0 if pair == 0 else 1 + chip]
@@ -173,6 +173,12 @@
         to_core0.start()
 
     issue(0, window)
+
+    for d in line_order:
+        pl.semaphore_signal(known, inc=1, device_id=plane_device(around(0, d)),
+                            device_id_type=pl.DeviceIdType.MESH)
+    turn(1)
+    pl.semaphore_wait(known, ny - 1)
 
     @pl.when(jnp.logical_and(first_col, head_core))
     def _():
@@ -188,7 +194,6 @@
     def _():
         to_core0.wait_send()
 
-    turn(1)
     got[:, :, own_cols:, :] = jnp.zeros((2, rows_n, LANES - own_cols, LANES), F32)
     for pair in range(2):
         got[pair, row, 0:own_cols, :] = turned[pair, pl.ds(pl.multiple_of(row * own_cols, 8), own_cols), :]
@@ -533,6 +538,7 @@
         pltpu.VMEM((nz, 2, slab // rows_n, LANES), F32),
         dma((2,)), dma((8,)), dma((1 + nz,)), dma((6,)), dma((6,)), dma((3,)), dma((3,)),
         dma((4,)), dma((4 + nx,)), dma((1,)),
+        pltpu.SemaphoreType.REGULAR,
     ]
     vmem, anywhere = pl.BlockSpec(memory_space=pltpu.VMEM), pl.BlockSpec(memory_space=pl.ANY)
     blocks = pl.pallas_call(

time: 88.6 us -> 86.8 us (0.980)
  Pallas kernels: 88.5 us -> 86.6 us
    pallas_call x1, Pallas kernels: 86.8 us -> 84.9 us  [body(): pl.pallas_call(functools.partial(kernel, (nx, ny, nz, piece, head_piece,...]
where the time goes in v6:
time: 86.8 us; the launch traced here: 86.6 us
  Pallas kernels  86.6 us (100%)
    pallas_call x1, Pallas kernels, body(): pl.pallas_call(functools.partial(kernel, (nx, ny, nz, piece, head_piece,...  84.9 us

profile of v6, /device:TPU:1, one launch (start us, length us, event | category | flops | bytes accessed | tf_op | source)
XLA Modules:
  0.0 86.6 jit_solution(3823313138480656590)
XLA Ops:
  0.0 84.9 %shard_map.64.blocks = f32[8,2,12,128]{3,2,1,0:T(8,128)} custom-call(f32[64,1664]{1,0:T(8,128)} %refs_0_.1, f32[64,1664]{1,0:T(8,128)} %refs_1_.1, f32[64,1664]{1,0:T(8,128)} %refs_2_.1, f32[64,1664]{1,0:T(8,128)} %refs_3_.1, f32[1,1024]{1,0:T(1,128)} %bitcast.2, f32[1,1024]{1,0:T(1,128)} %bitcast.3), custom_call_target="tpu_custom_call" | custom-call | flops 12884901888 | bytes 2097152 | tf_op jit(solution)/shard_map/pallas_call | solution.py:544
  84.9 1.6 %shard_map.65 = f32[12,1664]{1,0:T(8,128)} custom-call(f32[8,2,12,128]{3,2,1,0:T(8,128)} %shard_map.64.blocks), custom_call_target="tpu_custom_call" | custom-call | tf_op jit(solution)/shard_map/pallas_call | solution.py:554

commit v7 on v6

--- a/solution.py
+++ b/solution.py
@@ -268,9 +268,9 @@
                     third[...] = third[...] + through(heads[2, :, here], slab, high, rest, dot_nt)
             for at, value in ((0, first.T), (LANES, -second.T)):
                 high, rest = split(value)
-                lhs[here, at:at + LANES] = high
-                lhs[here, 256 + at:256 + at + LANES] = rest
-                lhs[here, 512 + at:512 + at + LANES] = high
+                lhs[pair, here, at:at + LANES] = high
+                lhs[pair, here, 256 + at:256 + at + LANES] = rest
+                lhs[pair, here, 512 + at:512 + at + LANES] = high
 
         def arrive(i):
             d = nz // 2 + ((i + 1) // 2) * (1 - 2 * (i % 2))
@@ -291,17 +291,21 @@
         low[0:slab, :] = high
         low[slab:, :] = rest
 
-    def columns(pair, j):
+    def symmetric(pair, j):
         here = slice(j * block, (j + 1) * block)
         right = rhs[pair, :, here]
         step = min(256, block)
         for start in range(block * j, keep, step):
             there = slice(start, start + step)
-            value = factor[there, here] * dot_nn(lhs[there, :], right)
-            sym_high[there, here], sym_rest[there, here] = split(value)
+            value = factor[there, here] * dot_nn(lhs[pair, there, :], right)
+            sym_high[pair, there, here], sym_rest[pair, there, here] = split(value)
             if start >= block * (j + 1):
-                sym_high[here, there], sym_rest[here, there] = split(value.T)
-        total = through(heads[pair], slab, sym_high[:, here], sym_rest[:, here], dot_nn)
+                sym_high[pair, here, there], sym_rest[pair, here, there] = split(value.T)
+
+    def columns(pair, j):
+        here = slice(j * block, (j + 1) * block)
+        right = rhs[pair, :, here]
+        total = through(heads[pair], slab, sym_high[pair, :, here], sym_rest[pair, :, here], dot_nn)
         at = LANES * pair
         outer = through(low[...], slab, right[at:at + LANES], right[512 + at:512 + at + LANES], dot_nn)
         if pair == 0:
@@ -315,6 +319,8 @@
                     w_part[h, (j * (block // LANES) + t) * groups + g] = total[start:start + piece, t * LANES:(t + 1) * LANES]
 
     prepare(0)
+    for j in range(2):
+        symmetric(0, j)
 
     to_core1 = remote(head_all, head_all, core_send.at[1], core_recv.at[1], (other, col))
 
@@ -401,6 +407,7 @@
                     rs(j, dx, i).start()
 
     for j in range(keep // block):
+        symmetric(1, j)
         columns(1, j)
         w_swap(j).start()
         sent.append(w_swap(j).wait_send)
@@ -505,7 +512,7 @@
         pltpu.VMEM((2, LANES, width), F32),
         pltpu.VMEM((2, width, LANES), F32),
         pltpu.VMEM((2, rows_n, LANES, LANES), F32),
-        pltpu.VMEM((keep, 768), BF16),
+        pltpu.VMEM((2, keep, 768), BF16),
         pltpu.VMEM((2, 768, keep), BF16),
         pltpu.VMEM((LANES, keep), F32),
         pltpu.VMEM((LANES, keep), F32),
@@ -527,8 +534,8 @@
         pltpu.VMEM((nz, piece, LANES), F32),
         pltpu.VMEM((piece, LANES), F32),
         pltpu.VMEM(pieces, F32),
-        pltpu.VMEM((keep, keep), BF16),
-        pltpu.VMEM((keep, keep), BF16),
+        pltpu.VMEM((2, keep, keep), BF16),
+        pltpu.VMEM((2, keep, keep), BF16),
         pltpu.VMEM((2 * slab, LANES), BF16),
         pltpu.VMEM((slab, LANES), F32),
         pltpu.VMEM((half, LANES), F32),

time: 86.8 us -> 85.8 us (0.988)
  Pallas kernels: 86.6 us -> 85.6 us
    pallas_call x1, Pallas kernels: 84.9 us -> 83.9 us  [body(): pl.pallas_call(functools.partial(kernel, (nx, ny, nz, piece, head_piece,...]
where the time goes in v7:
time: 85.8 us; the launch traced here: 85.6 us
  Pallas kernels  85.6 us (100%)
    pallas_call x1, Pallas kernels, body(): pl.pallas_call(functools.partial(kernel, (nx, ny, nz, piece, head_piece,...  83.9 us

profile of v7, /device:TPU:1, one launch (start us, length us, event | category | flops | bytes accessed | tf_op | source)
XLA Modules:
  0.0 85.6 jit_solution(10664467675503012810)
XLA Ops:
  0.0 83.9 %shard_map.64.blocks = f32[8,2,12,128]{3,2,1,0:T(8,128)} custom-call(f32[64,1664]{1,0:T(8,128)} %refs_0_.1, f32[64,1664]{1,0:T(8,128)} %refs_1_.1, f32[64,1664]{1,0:T(8,128)} %refs_2_.1, f32[64,1664]{1,0:T(8,128)} %refs_3_.1, f32[1,1024]{1,0:T(1,128)} %bitcast.2, f32[1,1024]{1,0:T(1,128)} %bitcast.3), custom_call_target="tpu_custom_call" | custom-call | flops 12884901888 | bytes 2097152 | tf_op jit(solution)/shard_map/pallas_call | solution.py:551
  83.9 1.6 %shard_map.65 = f32[12,1664]{1,0:T(8,128)} custom-call(f32[8,2,12,128]{3,2,1,0:T(8,128)} %shard_map.64.blocks), custom_call_target="tpu_custom_call" | custom-call | tf_op jit(solution)/shard_map/pallas_call | solution.py:561

commit v8 on v7

--- a/solution.py
+++ b/solution.py
@@ -438,7 +438,6 @@
     high, rest = split(p_other[...])
     last_high[LANES:, :] = high
     last_rest[LANES:, :] = rest
-    last_left[...] = jnp.zeros(last_left.shape, BF16)
 
     def send_out(i):
         return remote(out_src.at[i], out_buf.at[z], sum_send.at[3], sum_recv.at[3], (core * nz + i, col))
@@ -457,9 +456,8 @@
 
         for zb in range(nz):
             here = slice(zb * LANES, (zb + 1) * LANES)
-            high, rest = split(w_full[g * ny + 2 * (zb % (nz // 2)) + zb // (nz // 2)])
-            last_left[0:piece, here] = high
-            last_left[32:32 + piece, here] = rest
+            part = w_full[g * ny + 2 * (zb % (nz // 2)) + zb // (nz // 2)]
+            last_left[0:32, here], last_left[32:64, here] = split(jnp.pad(part, ((0, 32 - piece), (0, 0))))
         both = dot_nt(last_left[...], last_high[...])
         product = both[0:piece] + both[32:32 + piece] + dot_nt(last_left[0:32, :], last_rest[...])[0:piece]
         mine = product[:, :LANES] + third[pl.ds(pl.multiple_of(core * half + g * piece, 8), piece), :]

time: 85.8 us -> 85.8 us (level)
  no operation moved by 1% of the time
where the time goes in v8:
time: 85.8 us; the launch traced here: 85.6 us
  Pallas kernels  85.6 us (100%)
    pallas_call x1, Pallas kernels, body(): pl.pallas_call(functools.partial(kernel, (nx, ny, nz, piece, head_piece,...  83.9 us

profile of v8, /device:TPU:1, one launch (start us, length us, event | category | flops | bytes accessed | tf_op | source)
XLA Modules:
  0.0 85.6 jit_solution(1901646320898626411)
XLA Ops:
  0.0 83.9 %shard_map.64.blocks = f32[8,2,12,128]{3,2,1,0:T(8,128)} custom-call(f32[64,1664]{1,0:T(8,128)} %refs_0_.1, f32[64,1664]{1,0:T(8,128)} %refs_1_.1, f32[64,1664]{1,0:T(8,128)} %refs_2_.1, f32[64,1664]{1,0:T(8,128)} %refs_3_.1, f32[1,1024]{1,0:T(1,128)} %bitcast.2, f32[1,1024]{1,0:T(1,128)} %bitcast.3), custom_call_target="tpu_custom_call" | custom-call | flops 12884901888 | bytes 2097152 | tf_op jit(solution)/shard_map/pallas_call | solution.py:549
  83.9 1.6 %shard_map.65 = f32[12,1664]{1,0:T(8,128)} custom-call(f32[8,2,12,128]{3,2,1,0:T(8,128)} %shard_map.64.blocks), custom_call_target="tpu_custom_call" | custom-call | tf_op jit(solution)/shard_map/pallas_call | solution.py:559
